TPU v7x, 32 devices: a whole 2x2x4 slice. The times are simulated.
32 devices in a mesh: dp: 2 (over y), expert: 16 (over z, x, core).
Axes of the slice: x: 2, y: 2, z: 4, core: 2. Of those that a mesh axis runs over, the one named last changes fastest.
Arguments:
- tokens: bfloat16 [1024, 2048], P(('dp', 'expert')), may hold values from -6 to 6
- routes: int32 [1024, 8], P(('dp', 'expert')), may hold values from 0 to 15, all different within a row; in each aligned block of 32 rows (0 to 31, 32 to 63, ...) at most 32 rows name the same one
- cotangent: bfloat16 [1024, 2048], P(('dp', 'expert')), may hold values from -6 to 6
- router_weight: bfloat16 [2048, 16], replicated, may hold values from -0.375 to 0.375
- gate_weight: bfloat16 [16, 2048, 768], P('expert'), may hold values from -0.125 to 0.125
- up_weight: bfloat16 [16, 2048, 768], P('expert'), may hold values from -0.125 to 0.125
- down_weight: bfloat16 [16, 768, 2048], P('expert'), may hold values from -0.21875 to 0.21875
Outputs:
- layer_out: bfloat16 [1024, 2048], P(('dp', 'expert'))
- token_grad: bfloat16 [1024, 2048], P(('dp', 'expert'))
- gate_grad: bfloat16 [16, 2048, 768], P('expert', 'dp')
- up_grad: bfloat16 [16, 2048, 768], P('expert', 'dp')
- down_grad: bfloat16 [16, 768, 2048], P('expert', None, 'dp')
- router_grad: float32 [2048, 16], replicated
Inputs may be any that keep to these rules, and one draw needn't show every extreme that they name: `routes`: each row names 8 different experts. Among the 32 rows of one device no expert is named by more than 32 rows, and in some device's rows an expert is named by exactly 32 rows.
All inputs are finite; a program needn't handle non-finite values.
Results may differ from a plain program's by a relative error of at most 0.0061.
Values may be sent and summed in bfloat16 or wider, within the bound.
A program may use at most 128 MiB of HBM per device.

v0:
```python
import jax
import jax.numpy as jnp
from jax import lax
from jax.sharding import PartitionSpec as P


def silu_parts(gate_act):
    sigmoid_value = jax.nn.sigmoid(gate_act)
    act_value = gate_act * sigmoid_value
    act_slope = sigmoid_value * (1.0 + gate_act * (1.0 - sigmoid_value))
    return (act_value, act_slope)


def expert_forward(arrived, gate_weight, up_weight, down_weight):
    gate_act = jnp.einsum(
        "sjcd,jdf->sjcf", arrived, gate_weight, preferred_element_type=jnp.float32
    )
    up_act = jnp.einsum("sjcd,jdf->sjcf", arrived, up_weight, preferred_element_type=jnp.float32)
    act_value, act_slope = silu_parts(gate_act)
    hidden = (act_value * up_act).astype(jnp.bfloat16)
    expert_out = jnp.einsum(
        "sjcf,jfd->sjcd", hidden, down_weight, preferred_element_type=jnp.float32
    ).astype(jnp.bfloat16)
    return (expert_out, (up_act, act_value, act_slope, hidden))


def expert_backward(arrived_grads, stored, gate_weight, up_weight, down_weight):
    up_act, act_value, act_slope, hidden = stored
    hidden_grad = jnp.einsum(
        "sjcd,jfd->sjcf", arrived_grads, down_weight, preferred_element_type=jnp.float32
    )
    gate_part = (hidden_grad * up_act * act_slope).astype(jnp.bfloat16)
    up_part = (hidden_grad * act_value).astype(jnp.bfloat16)
    input_grad = (
        jnp.einsum("sjcf,jdf->sjcd", gate_part, gate_weight, preferred_element_type=jnp.float32)
        + jnp.einsum("sjcf,jdf->sjcd", up_part, up_weight, preferred_element_type=jnp.float32)
    ).astype(jnp.bfloat16)
    return (input_grad, gate_part, up_part)


def local_slots(tokens, routes, cotangent, router_weight, gate_weight, up_weight, down_weight):
    tok_rows, top_count = routes.shape
    model_width = tokens.shape[1]
    expert_count = router_weight.shape[1]
    local_count = gate_weight.shape[0]
    group_size = lax.axis_size("expert")
    capacity = min(tok_rows, 2 * tok_rows * top_count // expert_count)
    slot_total = expert_count * capacity
    buffer_shape = (group_size, local_count, capacity, model_width)
    logits = jnp.dot(tokens, router_weight, preferred_element_type=jnp.float32)
    exp_logits = jnp.exp(logits)
    probability = exp_logits / jnp.sum(exp_logits, axis=1, keepdims=True)
    chosen = (
        routes[:, :, None] == jnp.arange(expert_count, dtype=jnp.int32)[None, None, :]
    ).astype(jnp.int32)
    chosen_float = chosen.astype(jnp.float32)
    selected = jnp.sum(chosen_float * probability[:, None, :], axis=2)
    sel_total = jnp.sum(selected, axis=1, keepdims=True)
    combine = selected / sel_total
    per_token = jnp.sum(chosen, axis=1)
    before = jnp.tril(jnp.ones((tok_rows, tok_rows), jnp.float32), -1)
    earlier = jnp.dot(before, per_token.astype(jnp.float32)).astype(jnp.int32)
    slot_ids = jnp.sum(chosen * earlier[:, None, :], axis=2)
    flat_slot = routes * capacity + slot_ids
    match_map = (
        flat_slot[:, :, None] == jnp.arange(slot_total, dtype=jnp.int32)[None, None, :]
    ).astype(jnp.float32)
    presence = jnp.sum(match_map, axis=1)
    weight_map = jnp.sum(match_map * combine[:, :, None], axis=1)
    send_rows = (
        jnp.einsum(
            "tr,td->rd", presence.astype(jnp.bfloat16), tokens, preferred_element_type=jnp.float32
        )
        .astype(jnp.bfloat16)
        .reshape(buffer_shape)
    )
    send_grads = (
        jnp.einsum(
            "tr,td->rd", weight_map, cotangent.astype(jnp.float32), precision=lax.Precision.HIGHEST
        )
        .astype(jnp.bfloat16)
        .reshape(buffer_shape)
    )
    arrived = lax.all_to_all(send_rows, "expert", split_axis=0, concat_axis=0, tiled=True)
    expert_out, stored = expert_forward(arrived, gate_weight, up_weight, down_weight)
    returned = lax.all_to_all(expert_out, "expert", split_axis=0, concat_axis=0, tiled=True)
    arrived_grads = lax.all_to_all(send_grads, "expert", split_axis=0, concat_axis=0, tiled=True)
    input_grad, gate_part, up_part = expert_backward(
        arrived_grads, stored, gate_weight, up_weight, down_weight
    )
    returned_grads = lax.all_to_all(input_grad, "expert", split_axis=0, concat_axis=0, tiled=True)
    hidden = stored[3]
    gate_term = jnp.einsum("sjcd,sjcf->jdf", arrived, gate_part, preferred_element_type=jnp.float32)
    up_term = jnp.einsum("sjcd,sjcf->jdf", arrived, up_part, preferred_element_type=jnp.float32)
    down_term = jnp.einsum(
        "sjcf,sjcd->jfd", hidden, arrived_grads, preferred_element_type=jnp.float32
    )
    gate_sum, up_sum, down_sum = (
        lax.psum_scatter(gate_term, "dp", scatter_dimension=1, tiled=True),
        lax.psum_scatter(up_term, "dp", scatter_dimension=1, tiled=True),
        lax.psum_scatter(down_term, "dp", scatter_dimension=2, tiled=True),
    )
    gate_grad = gate_sum.astype(jnp.bfloat16)
    up_grad = up_sum.astype(jnp.bfloat16)
    down_grad = down_sum.astype(jnp.bfloat16)
    flat_index = flat_slot.reshape(-1)
    out_sel = jnp.take(returned.reshape(slot_total, model_width), flat_index, axis=0).reshape(
        tok_rows, top_count, model_width
    )
    grad_sel = jnp.take(
        returned_grads.reshape(slot_total, model_width), flat_index, axis=0
    ).reshape(tok_rows, top_count, model_width)
    layer_out = jnp.sum(combine[:, :, None] * out_sel.astype(jnp.float32), axis=1).astype(
        jnp.bfloat16
    )
    comb_grad = jnp.einsum("tkd,td->tk", out_sel, cotangent, preferred_element_type=jnp.float32)
    sel_grad = (comb_grad - jnp.sum(combine * comb_grad, axis=1, keepdims=True)) / sel_total
    prob_grad = jnp.sum(chosen_float * sel_grad[:, :, None], axis=1)
    logit_grad = probability * (prob_grad - jnp.sum(probability * prob_grad, axis=1, keepdims=True))
    router_term = jnp.einsum(
        "td,te->de", tokens.astype(jnp.float32), logit_grad, precision=lax.Precision.HIGHEST
    )
    router_grad = lax.psum(router_term, ("dp", "expert"))
    router_back = jnp.einsum(
        "te,de->td", logit_grad, router_weight.astype(jnp.float32), precision=lax.Precision.HIGHEST
    )
    token_grad = (jnp.sum(grad_sel.astype(jnp.float32), axis=1) + router_back).astype(jnp.bfloat16)
    return (layer_out, token_grad, gate_grad, up_grad, down_grad, router_grad)


def swap(array, bit):
    if bit == 0:
        return lax.ppermute(array, "dp", [(0, 1), (1, 0)])
    size = lax.axis_size("expert")
    return lax.ppermute(array, "expert", [(i, i ^ bit) for i in range(size)])


def local_dense(tokens, routes, cotangent, router_weight, gate_weight, up_weight, down_weight):
    tok_rows = tokens.shape[0]
    model_width = tokens.shape[1]
    expert_count = router_weight.shape[1]
    group_size = lax.axis_size("expert")
    dp_size = lax.axis_size("dp")
    dp_index = lax.axis_index("dp")
    expert_index = lax.axis_index("expert")
    gate_mat, up_mat, down_mat = gate_weight[0], up_weight[0], down_weight[0]
    logits = jnp.dot(tokens, router_weight, preferred_element_type=jnp.float32)
    exp_logits = jnp.exp(logits)
    probability = exp_logits / jnp.sum(exp_logits, axis=1, keepdims=True)
    chosen = jnp.sum(
        (routes[:, :, None] == jnp.arange(expert_count, dtype=jnp.int32)[None, None, :]).astype(
            jnp.float32
        ),
        axis=1,
    )
    selected = chosen * probability
    sel_total = jnp.sum(selected, axis=1, keepdims=True)
    combine = selected / sel_total
    bits = [1, 0, 2, 8, 4]
    ones = (1,) * len(bits)

    def gather(array, order):
        array = array.reshape(ones + array.shape)
        for bit in order:
            array = jnp.concatenate([array, swap(array, bit)], axis=bits.index(bit))
        return array.reshape((-1, array.shape[-1]))

    combine_all = gather(combine, (4, 8, 2, 0, 1))
    tokens_all = gather(tokens, (4, 8, 2, 0, 1))
    cot_all = gather(cotangent, (4, 8, 0, 2, 1))
    mine = (jnp.arange(expert_count, dtype=jnp.int32) == expert_index).astype(jnp.float32)
    scale = jnp.sum(combine_all * mine[None, :], axis=1, keepdims=True)
    gate_act = jnp.dot(tokens_all, gate_mat, preferred_element_type=jnp.float32)
    up_act = jnp.dot(tokens_all, up_mat, preferred_element_type=jnp.float32)
    raw_grad = lax.dot_general(
        cot_all, down_mat, (((1,), (1,)), ((), ())), preferred_element_type=jnp.float32
    )
    act_value, act_slope = silu_parts(gate_act)
    hidden = act_value * up_act
    comb_mine = jnp.sum(hidden * raw_grad, axis=1)
    scaled_hidden = (hidden * scale).astype(jnp.bfloat16)
    hidden_grad = raw_grad * scale
    gate_part = (hidden_grad * up_act * act_slope).astype(jnp.bfloat16)
    up_part = (hidden_grad * act_value).astype(jnp.bfloat16)

    def rows_of(array):
        quarter = array.reshape((2, 2, group_size * tok_rows // 2) + array.shape[1:])
        return quarter[:, 0].reshape((group_size * tok_rows,) + array.shape[1:])

    def scatter(term):
        term = term.reshape((2, 2, 2, 2, tok_rows, model_width))
        for bit in (1, 2, 8, 4):
            total = term[0].astype(jnp.float32) + swap(term[1], bit).astype(jnp.float32)
            term = total.astype(jnp.bfloat16)
        return total

    out_term = jnp.dot(
        rows_of(scaled_hidden), down_mat, preferred_element_type=jnp.float32
    ).astype(jnp.bfloat16)
    in_term = (
        lax.dot_general(
            rows_of(gate_part), gate_mat, (((1,), (1,)), ((), ())),
            preferred_element_type=jnp.float32,
        )
        + lax.dot_general(
            rows_of(up_part), up_mat, (((1,), (1,)), ((), ())),
            preferred_element_type=jnp.float32,
        )
    ).astype(jnp.bfloat16)
    layer_out = scatter(out_term).astype(jnp.bfloat16)
    in_sum = scatter(in_term)
    part_width = model_width // dp_size
    start = dp_index * part_width
    tokens_part = lax.dynamic_slice_in_dim(tokens_all, start, part_width, axis=1)
    cot_part = lax.dynamic_slice_in_dim(cot_all, start, part_width, axis=1)
    over_rows = (((0,), (0,)), ((), ()))
    gate_grad = lax.dot_general(
        tokens_part, gate_part, over_rows, preferred_element_type=jnp.float32
    ).astype(jnp.bfloat16)
    up_grad = lax.dot_general(
        tokens_part, up_part, over_rows, preferred_element_type=jnp.float32
    ).astype(jnp.bfloat16)
    down_grad = lax.dot_general(
        scaled_hidden, cot_part, over_rows, preferred_element_type=jnp.float32
    ).astype(jnp.bfloat16)
    comb = rows_of(comb_mine).reshape((2, 2, 2, 2, tok_rows, 1))
    places = []
    for step, bit in enumerate((1, 2, 8, 4)):
        comb = jnp.concatenate([comb[0], swap(comb[1], bit)], axis=-1)
        places = places + [p + bit for p in places] if step else [0, bit]
    columns = jnp.asarray(places, jnp.int32) ^ expert_index
    spread = (
        columns[:, None] == jnp.arange(expert_count, dtype=jnp.int32)[None, :]
    ).astype(jnp.float32)
    comb_grad = jnp.sum(comb[:, :, None] * spread[None], axis=1)
    sel_grad = (
        chosen * (comb_grad - jnp.sum(combine * comb_grad, axis=1, keepdims=True)) / sel_total
    )
    logit_grad = probability * (sel_grad - jnp.sum(probability * sel_grad, axis=1, keepdims=True))
    router_term = jnp.einsum(
        "td,te->de", tokens.astype(jnp.float32), logit_grad, precision=lax.Precision.HIGHEST
    )
    router_grad = router_term
    for bit in (1, 2, 0, 8, 4):
        router_grad = router_grad + swap(router_grad, bit)
    router_back = jnp.einsum(
        "te,de->td", logit_grad, router_weight.astype(jnp.float32), precision=lax.Precision.HIGHEST
    )
    token_grad = (in_sum + router_back).astype(jnp.bfloat16)
    return (layer_out, token_grad, gate_grad[None], up_grad[None], down_grad[None], router_grad)


def local(tokens, routes, cotangent, router_weight, gate_weight, up_weight, down_weight):
    tok_rows, top_count = routes.shape
    capacity = min(tok_rows, 2 * tok_rows * top_count // router_weight.shape[1])
    dense = (
        capacity == tok_rows
        and gate_weight.shape[0] == 1
        and lax.axis_size("dp") == 2
        and lax.axis_size("expert") == 16
    )
    plan = local_dense if dense else local_slots
    return plan(tokens, routes, cotangent, router_weight, gate_weight, up_weight, down_weight)


def solution(mesh):
    return jax.shard_map(
        local,
        mesh=mesh,
        in_specs=(
            P(("dp", "expert"), None),
            P(("dp", "expert"), None),
            P(("dp", "expert"), None),
            P(),
            P("expert", None, None),
            P("expert", None, None),
            P("expert", None, None),
        ),
        out_specs=(
            P(("dp", "expert"), None),
            P(("dp", "expert"), None),
            P("expert", "dp", None),
            P("expert", "dp", None),
            P("expert", None, "dp"),
            P(),
        ),
        check_vma=False,
    )
```

profile of v0, /device:TPU:1, one launch (start us, length us, event | category | flops | bytes accessed | tf_op | source)
XLA Modules:
  0.0 213.2 jit_solution(8400251895410504167)
XLA Ops:
  0.7 2.2 %collective-permute-start = (bf16[1,1,1,1,1,32,2048]{6,5,4,3,2,1,0:T(8,128)(2,1)}, bf16[1,1,1,1,1,32,2048]{6,5,4,3,2,1,0:T(8,128)(2,1)S(1)}, u32[]{:S(2)}, u32[]{:S(2)}) collective-permute-start(bf16[1,1,1,1,1,32,2048]{6,5,4,3,2,1,0:T(8,128)(2,1)} %bitcast.114), channel_id=1, source_target_pairs={{0,4},{1,5},{2,6},{3,7},{4,0},{5,1},{6,2},{7,3},{8,12},{9,13},{10,... | collective-permute-start | bytes 393224 | tf_op jit(solution)/shard_map/ppermute | solution.py:135
  2.9 3.4 %collective-permute-done = bf16[1,1,1,1,1,32,2048]{6,5,4,3,2,1,0:T(8,128)(2,1)S(1)} collective-permute-done((bf16[1,1,1,1,1,32,2048]{6,5,4,3,2,1,0:T(8,128)(2,1)}, bf16[1,1,1,1,1,32,2048]{6,5,4,3,2,1,0:T(8,128)(2,1)S(1)}, u32[]{:S(2)}, u32[]{:S(2)}) %collective-permute-start) | collective-permute-done | bytes 131104 | tf_op jit(solution)/shard_map/ppermute | solution.py:135
  7.3 2.2 %collective-permute-start.1 = (bf16[1,1,1,1,2,32,2048]{6,5,4,3,2,1,0:T(8,128)(2,1)S(1)}, bf16[1,1,1,1,2,32,2048]{6,5,4,3,2,1,0:T(8,128)(2,1)S(1)}, u32[]{:S(2)}, u32[]{:S(2)}) collective-permute-start(bf16[1,1,1,1,2,32,2048]{6,5,4,3,2,1,0:T(8,128)(2,1)S(1)} %pad_maximum_fusion.8), channel_id=1, source_target_pairs={{0,8},{1,9},{2,10},{3,11},{4,12},{5,13},{6,14},{7,15},{8,0},{9,1},... | collective-permute-start | bytes 786440 | tf_op jit(solution)/shard_map/ppermute | solution.py:135
  9.5 11.7 %collective-permute-done.1 = bf16[1,1,1,1,2,32,2048]{6,5,4,3,2,1,0:T(8,128)(2,1)S(1)} collective-permute-done((bf16[1,1,1,1,2,32,2048]{6,5,4,3,2,1,0:T(8,128)(2,1)S(1)}, bf16[1,1,1,1,2,32,2048]{6,5,4,3,2,1,0:T(8,128)(2,1)S(1)}, u32[]{:S(2)}, u32[]{:S(2)}) %collective-permute-start.1) | collective-permute-done | bytes 262176 | tf_op jit(solution)/shard_map/ppermute | solution.py:135
  23.1 11.1 %collective-permute-done.2 = bf16[1,1,1,2,2,32,2048]{6,5,4,3,2,1,0:T(8,128)(2,1)S(1)} collective-permute-done((bf16[1,1,1,2,2,32,2048]{6,5,4,3,2,1,0:T(8,128)(2,1)S(1)}, bf16[1,1,1,2,2,32,2048]{6,5,4,3,2,1,0:T(8,128)(2,1)S(1)}, u32[]{:S(2)}, u32[]{:S(2)}) %collective-permute-start.2) | collective-permute-done | bytes 524320 | tf_op jit(solution)/shard_map/ppermute | solution.py:135
  36.2 2.6 %collective-permute-start.14 = (bf16[1,1,1,1,1,32,2048]{6,5,4,3,2,1,0:T(8,128)(2,1)S(1)}, bf16[1,1,1,1,1,32,2048]{6,5,4,3,2,1,0:T(8,128)(2,1)S(1)}, u32[]{:S(2)}, u32[]{:S(2)}) collective-permute-start(bf16[1,1,1,1,1,32,2048]{6,5,4,3,2,1,0:T(8,128)(2,1)S(1)} %bitcast.129), channel_id=1, source_target_pairs={{0,4},{1,5},{2,6},{3,7},{4,0},{5,1},{6,2},{7,3},{8,12},{9,13},{10,... | collective-permute-start | bytes 393224 | tf_op jit(solution)/shard_map/ppermute | solution.py:135
  38.8 2.6 %collective-permute-done.14 = bf16[1,1,1,1,1,32,2048]{6,5,4,3,2,1,0:T(8,128)(2,1)S(1)} collective-permute-done((bf16[1,1,1,1,1,32,2048]{6,5,4,3,2,1,0:T(8,128)(2,1)S(1)}, bf16[1,1,1,1,1,32,2048]{6,5,4,3,2,1,0:T(8,128)(2,1)S(1)}, u32[]{:S(2)}, u32[]{:S(2)}) %collective-permute-start.14) | collective-permute-done | bytes 131104 | tf_op jit(solution)/shard_map/ppermute | solution.py:135
  41.5 3.2 %collective-permute-start.15 = (bf16[1,1,1,1,2,32,2048]{6,5,4,3,2,1,0:T(8,128)(2,1)S(1)}, bf16[1,1,1,1,2,32,2048]{6,5,4,3,2,1,0:T(8,128)(2,1)S(1)}, u32[]{:S(2)}, u32[]{:S(2)}) collective-permute-start(bf16[1,1,1,1,2,32,2048]{6,5,4,3,2,1,0:T(8,128)(2,1)S(1)} %pad_maximum_fusion.9), channel_id=1, source_target_pairs={{0,8},{1,9},{2,10},{3,11},{4,12},{5,13},{6,14},{7,15},{8,0},{9,1},... | collective-permute-start | bytes 786440 | tf_op jit(solution)/shard_map/ppermute | solution.py:135
  44.7 11.1 %collective-permute-done.15 = bf16[1,1,1,1,2,32,2048]{6,5,4,3,2,1,0:T(8,128)(2,1)S(1)} collective-permute-done((bf16[1,1,1,1,2,32,2048]{6,5,4,3,2,1,0:T(8,128)(2,1)S(1)}, bf16[1,1,1,1,2,32,2048]{6,5,4,3,2,1,0:T(8,128)(2,1)S(1)}, u32[]{:S(2)}, u32[]{:S(2)}) %collective-permute-start.15) | collective-permute-done | bytes 262176 | tf_op jit(solution)/shard_map/ppermute | solution.py:135
  59.4 5.2 %collective-permute-start.4 = (bf16[1,2,2,2,2,32,2048]{6,5,4,3,2,1,0:T(8,128)(2,1)}, bf16[1,2,2,2,2,32,2048]{6,5,4,3,2,1,0:T(8,128)(2,1)}, u32[]{:S(2)}, u32[]{:S(2)}) collective-permute-start(bf16[1,2,2,2,2,32,2048]{6,5,4,3,2,1,0:T(8,128)(2,1)} %pad_maximum_fusion.2), channel_id=1, source_target_pairs={{0,1},{1,0},{2,3},{3,2},{4,5},{5,4},{6,7},{7,6},{8,9},{9,8},{10,11... | collective-permute-start | bytes 6291464 | tf_op jit(solution)/shard_map/ppermute | solution.py:135
  64.8 5.1 %collective-permute-done.16 = bf16[1,1,1,2,2,32,2048]{6,5,4,3,2,1,0:T(8,128)(2,1)S(1)} collective-permute-done((bf16[1,1,1,2,2,32,2048]{6,5,4,3,2,1,0:T(8,128)(2,1)S(1)}, bf16[1,1,1,2,2,32,2048]{6,5,4,3,2,1,0:T(8,128)(2,1)S(1)}, u32[]{:S(2)}, u32[]{:S(2)}) %collective-permute-start.16) | collective-permute-done | bytes 524320 | tf_op jit(solution)/shard_map/ppermute | solution.py:133
  73.1 2.2 %collective-permute-start.5 = (f32[1,1,1,1,1,32,16]{5,6,4,3,2,1,0:T(8,128)S(1)}, f32[1,1,1,1,1,32,16]{5,6,4,3,2,1,0:T(8,128)S(1)}, u32[]{:S(2)}, u32[]{:S(2)}) collective-permute-start(f32[1,1,1,1,1,32,16]{5,6,4,3,2,1,0:T(8,128)S(1)} %fusion.62), channel_id=1, source_target_pairs={{0,4},{1,5},{2,6},{3,7},{4,0},{5,1},{6,2},{7,3},{8,12},{9,13},{10,... | collective-permute-start | bytes 6152 | tf_op jit(solution)/shard_map/ppermute | solution.py:135
  76.4 3.5 %collective-permute-start.6 = (f32[1,1,1,1,2,32,16]{5,6,4,3,2,1,0:T(8,128)S(1)}, f32[1,1,1,1,2,32,16]{5,6,4,3,2,1,0:T(8,128)S(1)}, u32[]{:S(2)}, u32[]{:S(2)}) collective-permute-start(f32[1,1,1,1,2,32,16]{5,6,4,3,2,1,0:T(8,128)S(1)} %pad_maximum_fusion.13), channel_id=1, source_target_pairs={{0,8},{1,9},{2,10},{3,11},{4,12},{5,13},{6,14},{7,15},{8,0},{9,1},... | collective-permute-start | bytes 12296 | tf_op jit(solution)/shard_map/ppermute | solution.py:135
  82.5 12.8 %collective-permute-done.7 = f32[1,1,1,2,2,32,16]{5,6,4,3,2,1,0:T(8,128)} collective-permute-done((f32[1,1,1,2,2,32,16]{5,6,4,3,2,1,0:T(8,128)}, f32[1,1,1,2,2,32,16]{5,6,4,3,2,1,0:T(8,128)}, u32[]{:S(2)}, u32[]{:S(2)}) %collective-permute-start.7) | collective-permute-done | bytes 8224 | tf_op jit(solution)/shard_map/ppermute | solution.py:135
  100.0 4.4 %collective-permute-start.9 = (f32[1,2,2,2,2,32,16]{5,6,4,3,2,1,0:T(8,128)S(1)}, f32[1,2,2,2,2,32,16]{5,6,4,3,2,1,0:T(8,128)S(1)}, u32[]{:S(2)}, u32[]{:S(2)}) collective-permute-start(f32[1,2,2,2,2,32,16]{5,6,4,3,2,1,0:T(8,128)S(1)} %pad_maximum_fusion.10), channel_id=1, source_target_pairs={{0,1},{1,0},{2,3},{3,2},{4,5},{5,4},{6,7},{7,6},{8,9},{9,8},{10,11... | collective-permute-start | bytes 98312 | tf_op jit(solution)/shard_map/ppermute | solution.py:135
  110.0 2.0 pad_maximum_fusion
  112.1 3.4 %fusion.10 = f32[1024,768]{1,0:T(8,128)S(1)} fusion(bf16[1024,2048]{1,0:T(8,128)(2,1)S(1)} %bitcast.120, bf16[1,2048,768]{2,1,0:T(8,128)(2,1)S(1)} %copy-done.39), kind=kOutput, calls=%fused_computation.13 | convolution fusion | flops 3221225472 | bytes 10485760 | tf_op jit(solution)/shard_map/dot_general | solution.py:173
  115.6 3.4 %fusion.6 = f32[1024,768]{1,0:T(8,128)S(1)} fusion(bf16[1024,2048]{1,0:T(8,128)(2,1)S(1)} %bitcast.121, bf16[1,2048,768]{2,1,0:T(8,128)(2,1)S(1)} %copy-done.38), kind=kOutput, calls=%fused_computation.9 | convolution fusion | flops 3221225472 | bytes 10485760 | tf_op jit(solution)/shard_map/dot_general | solution.py:174
  120.7 6.5 %multiply_reduce_fusion = (f32[1024]{0:T(1024)S(1)}, bf16[1024,768]{1,0:T(8,128)(2,1)}, bf16[1024,768]{1,0:T(8,128)(2,1)}, bf16[1024,768]{1,0:T(8,128)(2,1)}) fusion(f32[1024,768]{1,0:T(8,128)S(1)} %fusion.6, f32[1024,768]{1,0:T(8,128)S(1)} %fusion.10, f32[1024]{0:T(1024)S(1)} %mul.85, bf16[1024,2048]{1,0:T(8,128)(2,1)S(1)} %bitcast.124, ...), kind=kOutput, calls=%fused_computation.15 | convolution fusion | flops 3236166656 | bytes 18358272 | tf_op jit(solution)/shard_map/dot_general | solution.py:175
  130.4 3.9 %fusion.4 = f32[512,2048]{1,0:T(8,128)S(1)} fusion(bf16[512,768]{1,0:T(8,128)(2,1)S(1)} %bitcast.138, bf16[1,2048,768]{2,1,0:T(8,128)(2,1)} %param.13), kind=kOutput, calls=%fused_computation.7 | convolution fusion | flops 1610612736 | bytes 8126464 | tf_op jit(solution)/shard_map/dot_general | solution.py:205
  137.8 3.9 %collective-permute-start.26 = (f32[32,8]{0,1:T(8,128)S(1)}, f32[32,8]{0,1:T(8,128)S(1)}, u32[]{:S(2)}, u32[]{:S(2)}) collective-permute-start(f32[32,8]{0,1:T(8,128)S(1)} %get-tuple-element.21), channel_id=1, source_target_pairs={{0,4},{1,5},{2,6},{3,7},{4,0},{5,1},{6,2},{7,3},{8,12},{9,13},{10,... | collective-permute-start | bytes 3080 | tf_op jit(solution)/shard_map/ppermute | solution.py:135
  147.2 4.7 %collective-permute-done.28 = f32[2048,16]{0,1:T(8,128)S(1)} collective-permute-done((f32[2048,16]{0,1:T(8,128)S(1)}, f32[2048,16]{0,1:T(8,128)S(1)}, u32[]{:S(2)}, u32[]{:S(2)}) %collective-permute-start.28) | collective-permute-done | bytes 131104 | tf_op jit(solution)/shard_map/ppermute | solution.py:135
  153.2 3.0 %fusion.35 = bf16[1,768,1024]{2,1,0:T(8,128)(2,1)} fusion(bf16[1024,768]{1,0:T(8,128)(2,1)S(1)} %copy-done.22, bf16[1024,2048]{1,0:T(8,128)(2,1)S(1)} %bitcast.125, s32[]{:T(128)S(6)} %select_n.4), kind=kOutput, calls=%fused_computation.38 | convolution fusion | flops 1611399168 | bytes 5242884 | tf_op jit(solution)/shard_map/dot_general | solution.py:223
  156.2 2.3 %collective-permute-start.30 = (f32[2048,16]{0,1:T(8,128)S(1)}, f32[2048,16]{0,1:T(8,128)S(1)}, u32[]{:S(2)}, u32[]{:S(2)}) collective-permute-start(f32[2048,16]{0,1:T(8,128)S(1)} %add.70), channel_id=1, source_target_pairs={{0,8},{1,9},{2,10},{3,11},{4,12},{5,13},{6,14},{7,15},{8,0},{9,1},... | collective-permute-start | bytes 393224 | tf_op jit(solution)/shard_map/ppermute | solution.py:135
  158.5 3.0 %fusion.38 = bf16[1,1024,768]{2,1,0:T(8,128)(2,1)} fusion(bf16[1024,768]{1,0:T(8,128)(2,1)S(1)} %copy-done.21, bf16[1024,2048]{1,0:T(8,128)(2,1)S(1)} %bitcast.122, s32[]{:T(128)S(6)} %select_n.4), kind=kOutput, calls=%fused_computation.39 | convolution fusion | flops 1611399168 | bytes 5242884 | tf_op jit(solution)/shard_map/dot_general | solution.py:220
  165.4 3.0 %fusion.41 = bf16[1,1024,768]{2,1,0:T(8,128)(2,1)} fusion(bf16[1024,768]{1,0:T(8,128)(2,1)S(1)} %copy-done.20, bf16[1024,2048]{1,0:T(8,128)(2,1)S(1)} %bitcast.123, s32[]{:T(128)S(6)} %select_n.4), kind=kOutput, calls=%fused_computation.40 | convolution fusion | flops 1611399168 | bytes 5242884 | tf_op jit(solution)/shard_map/dot_general | solution.py:217
  171.7 8.9 %collective-permute-done.20 = bf16[2,2,32,2048]{3,2,1,0:T(8,128)(2,1)S(1)} collective-permute-done((bf16[2,2,32,2048]{3,2,1,0:T(8,128)(2,1)S(1)}, bf16[2,2,32,2048]{3,2,1,0:T(8,128)(2,1)S(1)}, u32[]{:S(2)}, u32[]{:S(2)}) %collective-permute-start.20) | collective-permute-done | bytes 524320 | tf_op jit(solution)/shard_map/ppermute | solution.py:135
  180.7 3.8 %collective-permute-start.21 = (bf16[2,32,2048]{2,1,0:T(8,128)(2,1)S(1)}, bf16[2,32,2048]{2,1,0:T(8,128)(2,1)S(1)}, u32[]{:S(2)}, u32[]{:S(2)}) collective-permute-start(bf16[2,32,2048]{2,1,0:T(8,128)(2,1)S(1)} %slice_bitcast_fusion.4), channel_id=1, source_target_pairs={{0,8},{1,9},{2,10},{3,11},{4,12},{5,13},{6,14},{7,15},{8,0},{9,1},... | collective-permute-start | bytes 786440 | tf_op jit(solution)/shard_map/ppermute | solution.py:135
  184.5 7.3 %collective-permute-done.11 = bf16[2,2,32,2048]{3,2,1,0:T(8,128)(2,1)S(1)} collective-permute-done((bf16[2,2,32,2048]{3,2,1,0:T(8,128)(2,1)S(1)}, bf16[2,2,32,2048]{3,2,1,0:T(8,128)(2,1)S(1)}, u32[]{:S(2)}, u32[]{:S(2)}) %collective-permute-start.11) | collective-permute-done | bytes 524320 | tf_op jit(solution)/shard_map/ppermute | solution.py:135
  191.9 3.8 %collective-permute-start.12 = (bf16[2,32,2048]{2,1,0:T(8,128)(2,1)S(1)}, bf16[2,32,2048]{2,1,0:T(8,128)(2,1)S(1)}, u32[]{:S(2)}, u32[]{:S(2)}) collective-permute-start(bf16[2,32,2048]{2,1,0:T(8,128)(2,1)S(1)} %slice_bitcast_fusion.6), channel_id=1, source_target_pairs={{0,8},{1,9},{2,10},{3,11},{4,12},{5,13},{6,14},{7,15},{8,0},{9,1},... | collective-permute-start | bytes 786440 | tf_op jit(solution)/shard_map/ppermute | solution.py:135
  195.9 12.1 %collective-permute-done.12 = bf16[2,32,2048]{2,1,0:T(8,128)(2,1)S(1)} collective-permute-done((bf16[2,32,2048]{2,1,0:T(8,128)(2,1)S(1)}, bf16[2,32,2048]{2,1,0:T(8,128)(2,1)S(1)}, u32[]{:S(2)}, u32[]{:S(2)}) %collective-permute-start.12) | collective-permute-done | bytes 262176 | tf_op jit(solution)/shard_map/ppermute | solution.py:135
  209.2 3.3 %collective-permute-done.13 = bf16[32,2048]{1,0:T(8,128)(2,1)S(1)} collective-permute-done((bf16[32,2048]{1,0:T(8,128)(2,1)S(1)}, bf16[32,2048]{1,0:T(8,128)(2,1)S(1)}, u32[]{:S(2)}, u32[]{:S(2)}) %collective-permute-start.13) | collective-permute-done | bytes 131104 | tf_op jit(solution)/shard_map/ppermute | solution.py:135
  (182 shorter events, 50.0 us)
Async XLA Ops:
  0.7 5.6 %collective-permute-start = (bf16[1,1,1,1,1,32,2048]{6,5,4,3,2,1,0:T(8,128)(2,1)}, bf16[1,1,1,1,1,32,2048]{6,5,4,3,2,1,0:T(8,128)(2,1)S(1)}, u32[]{:S(2)}, u32[]{:S(2)}) collective-permute-start(bf16[1,1,1,1,1,32,2048]{6,5,4,3,2,1,0:T(8,128)(2,1)} %bitcast.114), channel_id=1, source_target_pairs={{0,4},{1,5},{2,6},{3,7},{4,0},{5,1},{6,2},{7,3},{8,12},{9,13},{10,... | collective-permute-start | bytes 393224 | tf_op jit(solution)/shard_map/ppermute | solution.py:135
  7.3 13.9 %collective-permute-start.1 = (bf16[1,1,1,1,2,32,2048]{6,5,4,3,2,1,0:T(8,128)(2,1)S(1)}, bf16[1,1,1,1,2,32,2048]{6,5,4,3,2,1,0:T(8,128)(2,1)S(1)}, u32[]{:S(2)}, u32[]{:S(2)}) collective-permute-start(bf16[1,1,1,1,2,32,2048]{6,5,4,3,2,1,0:T(8,128)(2,1)S(1)} %pad_maximum_fusion.8), channel_id=1, source_target_pairs={{0,8},{1,9},{2,10},{3,11},{4,12},{5,13},{6,14},{7,15},{8,0},{9,1},... | collective-permute-start | bytes 786440 | tf_op jit(solution)/shard_map/ppermute | solution.py:135
  22.1 12.1 %collective-permute-start.2 = (bf16[1,1,1,2,2,32,2048]{6,5,4,3,2,1,0:T(8,128)(2,1)S(1)}, bf16[1,1,1,2,2,32,2048]{6,5,4,3,2,1,0:T(8,128)(2,1)S(1)}, u32[]{:S(2)}, u32[]{:S(2)}) collective-permute-start(bf16[1,1,1,2,2,32,2048]{6,5,4,3,2,1,0:T(8,128)(2,1)S(1)} %pad_maximum_fusion.6), channel_id=1, source_target_pairs={{0,2},{1,3},{2,0},{3,1},{4,6},{5,7},{6,4},{7,5},{8,10},{9,11},{10,... | collective-permute-start | bytes 1572872 | tf_op jit(solution)/shard_map/ppermute | solution.py:135
  35.4 22.4 %collective-permute-start.3 = (bf16[1,1,2,2,2,32,2048]{6,5,4,3,2,1,0:T(8,128)(2,1)S(1)}, bf16[1,1,2,2,2,32,2048]{6,5,4,3,2,1,0:T(8,128)(2,1)S(1)}, u32[]{:S(2)}, u32[]{:S(2)}) collective-permute-start(bf16[1,1,2,2,2,32,2048]{6,5,4,3,2,1,0:T(8,128)(2,1)S(1)} %pad_maximum_fusion.4), channel_id=1, source_target_pairs={{0,16},{16,0},{1,17},{17,1},{2,18},{18,2},{3,19},{19,3},{4,20},{20... | collective-permute-start | bytes 3145736 | tf_op jit(solution)/shard_map/ppermute | solution.py:133
  36.2 5.3 %collective-permute-start.14 = (bf16[1,1,1,1,1,32,2048]{6,5,4,3,2,1,0:T(8,128)(2,1)S(1)}, bf16[1,1,1,1,1,32,2048]{6,5,4,3,2,1,0:T(8,128)(2,1)S(1)}, u32[]{:S(2)}, u32[]{:S(2)}) collective-permute-start(bf16[1,1,1,1,1,32,2048]{6,5,4,3,2,1,0:T(8,128)(2,1)S(1)} %bitcast.129), channel_id=1, source_target_pairs={{0,4},{1,5},{2,6},{3,7},{4,0},{5,1},{6,2},{7,3},{8,12},{9,13},{10,... | collective-permute-start | bytes 393224 | tf_op jit(solution)/shard_map/ppermute | solution.py:135
  41.5 14.3 %collective-permute-start.15 = (bf16[1,1,1,1,2,32,2048]{6,5,4,3,2,1,0:T(8,128)(2,1)S(1)}, bf16[1,1,1,1,2,32,2048]{6,5,4,3,2,1,0:T(8,128)(2,1)S(1)}, u32[]{:S(2)}, u32[]{:S(2)}) collective-permute-start(bf16[1,1,1,1,2,32,2048]{6,5,4,3,2,1,0:T(8,128)(2,1)S(1)} %pad_maximum_fusion.9), channel_id=1, source_target_pairs={{0,8},{1,9},{2,10},{3,11},{4,12},{5,13},{6,14},{7,15},{8,0},{9,1},... | collective-permute-start | bytes 786440 | tf_op jit(solution)/shard_map/ppermute | solution.py:135
  55.9 14.1 %collective-permute-start.16 = (bf16[1,1,1,2,2,32,2048]{6,5,4,3,2,1,0:T(8,128)(2,1)S(1)}, bf16[1,1,1,2,2,32,2048]{6,5,4,3,2,1,0:T(8,128)(2,1)S(1)}, u32[]{:S(2)}, u32[]{:S(2)}) collective-permute-start(bf16[1,1,1,2,2,32,2048]{6,5,4,3,2,1,0:T(8,128)(2,1)S(1)} %pad_maximum_fusion.7), channel_id=1, source_target_pairs={{0,16},{16,0},{1,17},{17,1},{2,18},{18,2},{3,19},{19,3},{4,20},{20... | collective-permute-start | bytes 1572872 | tf_op jit(solution)/shard_map/ppermute | solution.py:133
  59.4 50.6 %collective-permute-start.4 = (bf16[1,2,2,2,2,32,2048]{6,5,4,3,2,1,0:T(8,128)(2,1)}, bf16[1,2,2,2,2,32,2048]{6,5,4,3,2,1,0:T(8,128)(2,1)}, u32[]{:S(2)}, u32[]{:S(2)}) collective-permute-start(bf16[1,2,2,2,2,32,2048]{6,5,4,3,2,1,0:T(8,128)(2,1)} %pad_maximum_fusion.2), channel_id=1, source_target_pairs={{0,1},{1,0},{2,3},{3,2},{4,5},{5,4},{6,7},{7,6},{8,9},{9,8},{10,11... | collective-permute-start | bytes 6291464 | tf_op jit(solution)/shard_map/ppermute | solution.py:135
  71.8 35.9 %collective-permute-start.17 = (bf16[1,2,1,2,2,32,2048]{6,5,4,3,2,1,0:T(8,128)(2,1)}, bf16[1,2,1,2,2,32,2048]{6,5,4,3,2,1,0:T(8,128)(2,1)}, u32[]{:S(2)}, u32[]{:S(2)}) collective-permute-start(bf16[1,2,1,2,2,32,2048]{6,5,4,3,2,1,0:T(8,128)(2,1)} %pad_maximum_fusion.5), channel_id=1, source_target_pairs={{0,2},{1,3},{2,0},{3,1},{4,6},{5,7},{6,4},{7,5},{8,10},{9,11},{10,... | collective-permute-start | bytes 3145736 | tf_op jit(solution)/shard_map/ppermute | solution.py:135
  73.1 3.2 %collective-permute-start.5 = (f32[1,1,1,1,1,32,16]{5,6,4,3,2,1,0:T(8,128)S(1)}, f32[1,1,1,1,1,32,16]{5,6,4,3,2,1,0:T(8,128)S(1)}, u32[]{:S(2)}, u32[]{:S(2)}) collective-permute-start(f32[1,1,1,1,1,32,16]{5,6,4,3,2,1,0:T(8,128)S(1)} %fusion.62), channel_id=1, source_target_pairs={{0,4},{1,5},{2,6},{3,7},{4,0},{5,1},{6,2},{7,3},{8,12},{9,13},{10,... | collective-permute-start | bytes 6152 | tf_op jit(solution)/shard_map/ppermute | solution.py:135
  76.4 4.6 %collective-permute-start.6 = (f32[1,1,1,1,2,32,16]{5,6,4,3,2,1,0:T(8,128)S(1)}, f32[1,1,1,1,2,32,16]{5,6,4,3,2,1,0:T(8,128)S(1)}, u32[]{:S(2)}, u32[]{:S(2)}) collective-permute-start(f32[1,1,1,1,2,32,16]{5,6,4,3,2,1,0:T(8,128)S(1)} %pad_maximum_fusion.13), channel_id=1, source_target_pairs={{0,8},{1,9},{2,10},{3,11},{4,12},{5,13},{6,14},{7,15},{8,0},{9,1},... | collective-permute-start | bytes 12296 | tf_op jit(solution)/shard_map/ppermute | solution.py:135
  82.2 13.1 %collective-permute-start.7 = (f32[1,1,1,2,2,32,16]{5,6,4,3,2,1,0:T(8,128)}, f32[1,1,1,2,2,32,16]{5,6,4,3,2,1,0:T(8,128)}, u32[]{:S(2)}, u32[]{:S(2)}) collective-permute-start(f32[1,1,1,2,2,32,16]{5,6,4,3,2,1,0:T(8,128)} %pad_maximum_fusion.12), channel_id=1, source_target_pairs={{0,2},{1,3},{2,0},{3,1},{4,6},{5,7},{6,4},{7,5},{8,10},{9,11},{10,... | collective-permute-start | bytes 24584 | tf_op jit(solution)/shard_map/ppermute | solution.py:135
  96.0 3.2 %collective-permute-start.8 = (f32[1,1,2,2,2,32,16]{5,6,4,3,2,1,0:T(8,128)S(1)}, f32[1,1,2,2,2,32,16]{5,6,4,3,2,1,0:T(8,128)S(1)}, u32[]{:S(2)}, u32[]{:S(2)}) collective-permute-start(f32[1,1,2,2,2,32,16]{5,6,4,3,2,1,0:T(8,128)S(1)} %pad_maximum_fusion.11), channel_id=1, source_target_pairs={{0,16},{16,0},{1,17},{17,1},{2,18},{18,2},{3,19},{19,3},{4,20},{20... | collective-permute-start | bytes 49160 | tf_op jit(solution)/shard_map/ppermute | solution.py:133
  100.0 5.4 %collective-permute-start.9 = (f32[1,2,2,2,2,32,16]{5,6,4,3,2,1,0:T(8,128)S(1)}, f32[1,2,2,2,2,32,16]{5,6,4,3,2,1,0:T(8,128)S(1)}, u32[]{:S(2)}, u32[]{:S(2)}) collective-permute-start(f32[1,2,2,2,2,32,16]{5,6,4,3,2,1,0:T(8,128)S(1)} %pad_maximum_fusion.10), channel_id=1, source_target_pairs={{0,1},{1,0},{2,3},{3,2},{4,5},{5,4},{6,7},{7,6},{8,9},{9,8},{10,11... | collective-permute-start | bytes 98312 | tf_op jit(solution)/shard_map/ppermute | solution.py:135
  109.6 9.5 %collective-permute-start.18 = (bf16[1,2,2,2,2,32,2048]{6,5,4,3,2,1,0:T(8,128)(2,1)S(1)}, bf16[1,2,2,2,2,32,2048]{6,5,4,3,2,1,0:T(8,128)(2,1)S(1)}, u32[]{:S(2)}, u32[]{:S(2)}) collective-permute-start(bf16[1,2,2,2,2,32,2048]{6,5,4,3,2,1,0:T(8,128)(2,1)S(1)} %pad_maximum_fusion.3), channel_id=1, source_target_pairs={{0,1},{1,0},{2,3},{3,2},{4,5},{5,4},{6,7},{7,6},{8,9},{9,8},{10,11... | collective-permute-start | bytes 6291464 | tf_op jit(solution)/shard_map/ppermute | solution.py:135
  127.3 1.7 collective-permute-start.23
  129.1 5.2 %collective-permute-start.24 = (f32[2,2,32,2]{2,3,1,0:T(2,128)S(1)}, f32[2,2,32,2]{2,3,1,0:T(2,128)S(1)}, u32[]{:S(2)}, u32[]{:S(2)}) collective-permute-start(f32[2,2,32,2]{2,3,1,0:T(2,128)S(1)} %get-tuple-element.25), channel_id=1, source_target_pairs={{0,2},{1,3},{2,0},{3,1},{4,6},{5,7},{6,4},{7,5},{8,10},{9,11},{10,... | collective-permute-start | bytes 3080 | tf_op jit(solution)/shard_map/ppermute | solution.py:135
  134.3 3.4 %collective-permute-start.25 = (f32[2,32,4]{1,2,0:T(4,128)S(1)}, f32[2,32,4]{1,2,0:T(4,128)S(1)}, u32[]{:S(2)}, u32[]{:S(2)}) collective-permute-start(f32[2,32,4]{1,2,0:T(4,128)S(1)} %get-tuple-element.23), channel_id=1, source_target_pairs={{0,8},{1,9},{2,10},{3,11},{4,12},{5,13},{6,14},{7,15},{8,0},{9,1},... | collective-permute-start | bytes 3080 | tf_op jit(solution)/shard_map/ppermute | solution.py:135
  137.8 5.3 %collective-permute-start.26 = (f32[32,8]{0,1:T(8,128)S(1)}, f32[32,8]{0,1:T(8,128)S(1)}, u32[]{:S(2)}, u32[]{:S(2)}) collective-permute-start(f32[32,8]{0,1:T(8,128)S(1)} %get-tuple-element.21), channel_id=1, source_target_pairs={{0,4},{1,5},{2,6},{3,7},{4,0},{5,1},{6,2},{7,3},{8,12},{9,13},{10,... | collective-permute-start | bytes 3080 | tf_op jit(solution)/shard_map/ppermute | solution.py:135
  141.9 27.2 %collective-permute-start.19 = (bf16[2,2,2,32,2048]{4,3,2,1,0:T(8,128)(2,1)S(1)}, bf16[2,2,2,32,2048]{4,3,2,1,0:T(8,128)(2,1)S(1)}, u32[]{:S(2)}, u32[]{:S(2)}) collective-permute-start(bf16[2,2,2,32,2048]{4,3,2,1,0:T(8,128)(2,1)S(1)} %bitcast.134), channel_id=1, source_target_pairs={{0,1},{1,0},{2,3},{3,2},{4,5},{5,4},{6,7},{7,6},{8,9},{9,8},{10,11... | collective-permute-start | bytes 3145736 | tf_op jit(solution)/shard_map/ppermute | solution.py:135
  143.5 3.2 %collective-permute-start.27 = (f32[2048,16]{0,1:T(8,128)S(1)}, f32[2048,16]{0,1:T(8,128)S(1)}, u32[]{:S(2)}, u32[]{:S(2)}) collective-permute-start(f32[2048,16]{0,1:T(8,128)S(1)} %convolution_bitcast_fusion), channel_id=1, source_target_pairs={{0,1},{1,0},{2,3},{3,2},{4,5},{5,4},{6,7},{7,6},{8,9},{9,8},{10,11... | collective-permute-start | bytes 393224 | tf_op jit(solution)/shard_map/ppermute | solution.py:135
  146.7 5.2 %collective-permute-start.28 = (f32[2048,16]{0,1:T(8,128)S(1)}, f32[2048,16]{0,1:T(8,128)S(1)}, u32[]{:S(2)}, u32[]{:S(2)}) collective-permute-start(f32[2048,16]{0,1:T(8,128)S(1)} %add.68), channel_id=1, source_target_pairs={{0,2},{1,3},{2,0},{3,1},{4,6},{5,7},{6,4},{7,5},{8,10},{9,11},{10,... | collective-permute-start | bytes 393224 | tf_op jit(solution)/shard_map/ppermute | solution.py:135
  151.9 4.3 %collective-permute-start.29 = (f32[2048,16]{0,1:T(8,128)S(1)}, f32[2048,16]{0,1:T(8,128)S(1)}, u32[]{:S(2)}, u32[]{:S(2)}) collective-permute-start(f32[2048,16]{0,1:T(8,128)S(1)} %add.69), channel_id=1, source_target_pairs={{0,16},{16,0},{1,17},{17,1},{2,18},{18,2},{3,19},{19,3},{4,20},{20... | collective-permute-start | bytes 393224 | tf_op jit(solution)/shard_map/ppermute | solution.py:133
  156.2 7.3 %collective-permute-start.30 = (f32[2048,16]{0,1:T(8,128)S(1)}, f32[2048,16]{0,1:T(8,128)S(1)}, u32[]{:S(2)}, u32[]{:S(2)}) collective-permute-start(f32[2048,16]{0,1:T(8,128)S(1)} %add.70), channel_id=1, source_target_pairs={{0,8},{1,9},{2,10},{3,11},{4,12},{5,13},{6,14},{7,15},{8,0},{9,1},... | collective-permute-start | bytes 393224 | tf_op jit(solution)/shard_map/ppermute | solution.py:135
  161.6 8.4 %collective-permute-start.10 = (bf16[2,2,2,32,2048]{4,3,2,1,0:T(8,128)(2,1)S(1)}, bf16[2,2,2,32,2048]{4,3,2,1,0:T(8,128)(2,1)S(1)}, u32[]{:S(2)}, u32[]{:S(2)}) collective-permute-start(bf16[2,2,2,32,2048]{4,3,2,1,0:T(8,128)(2,1)S(1)} %bitcast.135), channel_id=1, source_target_pairs={{0,1},{1,0},{2,3},{3,2},{4,5},{5,4},{6,7},{7,6},{8,9},{9,8},{10,11... | collective-permute-start | bytes 3145736 | tf_op jit(solution)/shard_map/ppermute | solution.py:135
  163.6 4.9 %collective-permute-start.31 = (f32[2048,16]{0,1:T(8,128)S(1)}, f32[2048,16]{0,1:T(8,128)S(1)}, u32[]{:S(2)}, u32[]{:S(2)}) collective-permute-start(f32[2048,16]{0,1:T(8,128)S(1)} %add.71), channel_id=1, source_target_pairs={{0,4},{1,5},{2,6},{3,7},{4,0},{5,1},{6,2},{7,3},{8,12},{9,13},{10,... | collective-permute-start | bytes 393224 | tf_op jit(solution)/shard_map/ppermute | solution.py:135
  169.6 10.9 %collective-permute-start.20 = (bf16[2,2,32,2048]{3,2,1,0:T(8,128)(2,1)S(1)}, bf16[2,2,32,2048]{3,2,1,0:T(8,128)(2,1)S(1)}, u32[]{:S(2)}, u32[]{:S(2)}) collective-permute-start(bf16[2,2,32,2048]{3,2,1,0:T(8,128)(2,1)S(1)} %slice_bitcast_fusion), channel_id=1, source_target_pairs={{0,2},{1,3},{2,0},{3,1},{4,6},{5,7},{6,4},{7,5},{8,10},{9,11},{10,... | collective-permute-start | bytes 1572872 | tf_op jit(solution)/shard_map/ppermute | solution.py:135
  170.4 21.4 %collective-permute-start.11 = (bf16[2,2,32,2048]{3,2,1,0:T(8,128)(2,1)S(1)}, bf16[2,2,32,2048]{3,2,1,0:T(8,128)(2,1)S(1)}, u32[]{:S(2)}, u32[]{:S(2)}) collective-permute-start(bf16[2,2,32,2048]{3,2,1,0:T(8,128)(2,1)S(1)} %slice_bitcast_fusion.2), channel_id=1, source_target_pairs={{0,2},{1,3},{2,0},{3,1},{4,6},{5,7},{6,4},{7,5},{8,10},{9,11},{10,... | collective-permute-start | bytes 1572872 | tf_op jit(solution)/shard_map/ppermute | solution.py:135
  180.7 15.0 %collective-permute-start.21 = (bf16[2,32,2048]{2,1,0:T(8,128)(2,1)S(1)}, bf16[2,32,2048]{2,1,0:T(8,128)(2,1)S(1)}, u32[]{:S(2)}, u32[]{:S(2)}) collective-permute-start(bf16[2,32,2048]{2,1,0:T(8,128)(2,1)S(1)} %slice_bitcast_fusion.4), channel_id=1, source_target_pairs={{0,8},{1,9},{2,10},{3,11},{4,12},{5,13},{6,14},{7,15},{8,0},{9,1},... | collective-permute-start | bytes 786440 | tf_op jit(solution)/shard_map/ppermute | solution.py:135
  191.9 16.1 %collective-permute-start.12 = (bf16[2,32,2048]{2,1,0:T(8,128)(2,1)S(1)}, bf16[2,32,2048]{2,1,0:T(8,128)(2,1)S(1)}, u32[]{:S(2)}, u32[]{:S(2)}) collective-permute-start(bf16[2,32,2048]{2,1,0:T(8,128)(2,1)S(1)} %slice_bitcast_fusion.6), channel_id=1, source_target_pairs={{0,8},{1,9},{2,10},{3,11},{4,12},{5,13},{6,14},{7,15},{8,0},{9,1},... | collective-permute-start | bytes 786440 | tf_op jit(solution)/shard_map/ppermute | solution.py:135
  195.8 12.4 %collective-permute-start.22 = (bf16[32,2048]{1,0:T(8,128)(2,1)S(1)}, bf16[32,2048]{1,0:T(8,128)(2,1)S(1)}, u32[]{:S(2)}, u32[]{:S(2)}) collective-permute-start(bf16[32,2048]{1,0:T(8,128)(2,1)S(1)} %slice_bitcast_fusion.8), channel_id=1, source_target_pairs={{0,4},{1,5},{2,6},{3,7},{4,0},{5,1},{6,2},{7,3},{8,12},{9,13},{10,... | collective-permute-start | bytes 393224 | tf_op jit(solution)/shard_map/ppermute | solution.py:135
  208.1 4.4 %collective-permute-start.13 = (bf16[32,2048]{1,0:T(8,128)(2,1)S(1)}, bf16[32,2048]{1,0:T(8,128)(2,1)S(1)}, u32[]{:S(2)}, u32[]{:S(2)}) collective-permute-start(bf16[32,2048]{1,0:T(8,128)(2,1)S(1)} %slice_bitcast_fusion.10), channel_id=1, source_target_pairs={{0,4},{1,5},{2,6},{3,7},{4,0},{5,1},{6,2},{7,3},{8,12},{9,13},{10,... | collective-permute-start | bytes 393224 | tf_op jit(solution)/shard_map/ppermute | solution.py:135
  (41 other events, 667.1 us)
where the time goes:
time: 215 us; the launch traced here: 213 us
  waiting for transfers between devices  102 us (47%)
  starting transfers between devices  55.2 us (26%)
  matrix products  31.4 us (15%)
  other arithmetic  19.1 us (9%)
  local copies, waits for them, and re-layouts  4.47 us (2%)
    ppermute x28, waiting for transfers between devices, swap(): return lax.ppermute(array, 'expert', [(i, i ^ bit) for i in range(size)])  93.6 us
    ppermute x28, starting transfers between devices, swap(): return lax.ppermute(array, 'expert', [(i, i ^ bit) for i in range(size)])  52.2 us
    concatenate x14, other arithmetic, gather(): array = jnp.concatenate([array, swap(array, bit)], axis=bits.index(bit))  13.4 us
    ppermute x4, waiting for transfers between devices, swap(): return lax.ppermute(array, 'dp', [(0, 1), (1, 0)])  8.03 us
    dot_general x1, matrix products, local_dense(): lax.dot_general(cot_all, down_mat, (((1,), (1,)), ((), ())), preferred_el...  6.54 us
  transfers between devices with their start and end apart: 32, of which 18 were waited for; matrix products, arithmetic and copies ran while one was open for 19% of the time, Pallas kernels for 0%

commit v1 on v0

--- a/solution.py
+++ b/solution.py
@@ -1,7 +1,513 @@
+import functools
+
 import jax
 import jax.numpy as jnp
 from jax import lax
+from jax.experimental import pallas as pl
+from jax.experimental.pallas import tpu as pltpu
 from jax.sharding import PartitionSpec as P
+
+MESH = pl.DeviceIdType.MESH
+NN = (((1,), (0,)), ((), ()))
+NT = (((1,), (1,)), ((), ()))
+TN = (((0,), (0,)), ((), ()))
+F32 = jnp.float32
+BF16 = jnp.bfloat16
+TILE = 256
+LANES = 128
+
+
+def dot(a, b, dims):
+    return lax.dot_general(a, b, dims, preferred_element_type=F32)
+
+
+def split3(value):
+    high = value.astype(BF16).astype(F32)
+    middle = (value - high).astype(BF16).astype(F32)
+    low = (value - high - middle).astype(BF16).astype(F32)
+    return high, middle, low
+
+
+class Book:
+    def __init__(self):
+        self.places = {}
+
+    def __call__(self, *key):
+        return self.places.setdefault(key, len(self.places))
+
+
+COPIES = 110
+
+
+def fused(
+    experts, tok_ref, routes_ref, cot_ref, router_ref, gate_hbm, up_hbm, down_hbm,
+    out_ref, tgrad_ref, gg_ref, ug_ref, dg_ref, rgrad_ref,
+    tok_all, cot_all, gate_w, up_w, down_w, gate_t, up_t, down_t,
+    hid, gpart, upart, out_p, in_p, core_o, core_i, x_o, x_i, z_o, z_i,
+    lgs, acc_g, acc_u, acc_d, small, load_sem, send_sem, recv_sem, lg_send, lg_recv,
+):
+    rows, width = tok_ref.shape
+    inner = gate_w.shape[1]
+    half = gg_ref.shape[0]
+    group = 4 * rows
+    dp = lax.axis_index("dp")
+    me = lax.axis_index("expert")
+    z, x, core = me // 4, (me // 2) % 2, me % 2
+    z_of = {0: z, 1: z + 1 - 2 * (z % 2), 2: (z + 2) % 4, 3: 3 - z}
+    middle_chip = (z + 1) % 4 >= 2
+
+    def device(ry=0, rz=0, rc=0, rx=0):
+        return (
+            1 - dp if ry else dp,
+            z_of[rz] * 4 + (1 - x if rx else x) * 2 + (1 - core if rc else core),
+        )
+
+    barrier = pltpu.get_barrier_semaphore()
+    others = [
+        (ry, rz, rc, rx) for ry in range(2) for rz in range(4) for rc in range(2) for rx in range(2)
+    ][1:]
+    for rel in others:
+        pl.semaphore_signal(barrier, inc=1, device_id=device(*rel), device_id_type=MESH)
+
+    loads = [
+        pltpu.make_async_copy(src, dst, load_sem.at[i])
+        for i, (src, dst) in enumerate(((down_hbm, down_w), (gate_hbm, gate_w), (up_hbm, up_w)))
+    ]
+    for load in loads:
+        load.start()
+
+    lane = lax.broadcasted_iota(jnp.int32, (rows, LANES), 1)
+    expert_lane = lane % experts
+    first = lane < experts
+    exp_logits = jnp.exp(dot(tok_ref[...], router_ref[...], NN))
+    masked = jnp.where(first, exp_logits, 0.0)
+    probability = exp_logits / jnp.sum(masked, axis=1, keepdims=True)
+    chosen = jnp.zeros((rows, LANES), F32)
+    for k in range(routes_ref.shape[1]):
+        chosen = chosen + (routes_ref[:, k : k + 1] == expert_lane).astype(F32)
+    selected = chosen * probability
+    sel_total = jnp.sum(jnp.where(first, selected, 0.0), axis=1, keepdims=True)
+    combine = selected / sel_total
+    part = lane // experts
+    high, mid, low = split3(combine)
+    aux = jnp.where(part == 0, high, jnp.where(part == 1, mid, jnp.where(part == 2, low, 0.0)))
+    tok_all[0, 0, 0, 0, :, :width] = tok_ref[...]
+    tok_all[0, 0, 0, 0, :, width:] = aux.astype(BF16)
+    cot_all[0, 0, 0, 0] = cot_ref[...]
+    small[0] = probability
+    small[1] = chosen
+    small[2] = combine
+    small[3] = jnp.broadcast_to(sel_total, (rows, LANES))
+
+    pl.semaphore_wait(barrier, len(others))
+
+    book = Book()
+    sent = []
+    blocks = (tok_all, cot_all)
+
+    def copy(src, dst, to, send_key, recv_key, keep=True):
+        made = pltpu.make_async_remote_copy(
+            src_ref=src, dst_ref=dst,
+            send_sem=send_sem.at[book("s", *send_key)], recv_sem=recv_sem.at[book(*recv_key)],
+            device_id=to, device_id_type=MESH,
+        )
+        made.start()
+        if keep:
+            sent.append(made)
+        return made
+
+    def arrived(dst, *key):
+        pltpu.make_async_remote_copy(
+            src_ref=dst, dst_ref=dst, send_sem=send_sem.at[0], recv_sem=recv_sem.at[book(*key)],
+            device_id=device(rc=1), device_id_type=MESH,
+        ).wait_recv()
+
+    later = []
+
+    def z_send(h, from_rel, to_rel, land):
+        a = blocks[h]
+        return copy(
+            a.at[0, from_rel, 0, 0], a.at[0, land, 0, 0], device(rz=to_rel),
+            ("z", from_rel, to_rel, h), ("z", land, h), keep=False,
+        )
+
+    def middle_only(*sends):
+        @pl.when(middle_chip)
+        def _():
+            for args in sends:
+                z_send(*args)
+
+        later.extend(sends)
+
+    def to_x(k, h):
+        a = blocks[h]
+        copy(a.at[0, k, 0, 0], a.at[0, k, 0, 1], device(rx=1), ("x", k, h), ("x", k, h))
+
+    def to_y(k, rx, h):
+        a = blocks[h]
+        copy(a.at[0, k, 0, rx], a.at[1, k, 0, rx], device(ry=1), ("y", k, rx, h), ("y", k, rx, h))
+
+    def to_core(ry, k, rx, h):
+        a = blocks[h]
+        copy(
+            a.at[ry, k, 0, rx], a.at[ry, k, 1, rx], device(rc=1), ("c", ry, k, rx, h), ("c", ry, k, rx, h)
+        )
+
+    def spread(k, h):
+        to_x(k, h)
+        to_core(0, k, 0, h)
+        to_y(k, 0, h)
+
+    def on_z(k, h):
+        if k == 1:
+            arrived(blocks[h].at[0, 1, 0, 0], "z", 1, h)
+            middle_only((h, 1, 3, 2))
+            spread(1, h)
+        elif k == 2:
+            @pl.when(middle_chip)
+            def _():
+                arrived(blocks[h].at[0, 3, 0, 0], "z", 3, h)
+                z_send(h, 3, 1, 2)
+                arrived(blocks[h].at[0, 2, 0, 0], "z", 2, h)
+                z_send(h, 2, 1, 3)
+
+            later.extend([(h, 3, 1, 2), (h, 2, 1, 3)])
+
+            @pl.when(jnp.logical_not(middle_chip))
+            def _():
+                arrived(blocks[h].at[0, 2, 0, 0], "z", 2, h)
+
+            spread(2, h)
+        else:
+            @pl.when(jnp.logical_not(middle_chip))
+            def _():
+                arrived(blocks[h].at[0, 3, 0, 0], "z", 3, h)
+
+            spread(3, h)
+
+    def on_x(k, h):
+        arrived(blocks[h].at[0, k, 0, 1], "x", k, h)
+        to_core(0, k, 1, h)
+        to_y(k, 1, h)
+
+    def on_y(k):
+        for h in range(2):
+            for rx in range(2):
+                arrived(blocks[h].at[1, k, 0, rx], "y", k, rx, h)
+                to_core(1, k, rx, h)
+
+    def on_core(ry, k):
+        for h in range(2):
+            for rx in range(2):
+                arrived(blocks[h].at[ry, k, 1, rx], "c", ry, k, rx, h)
+
+    group_lane = lax.broadcasted_iota(jnp.int32, (group, LANES), 1)
+
+    def backprop(ry, k):
+        at = ry * 4 + k
+        aux_rows = tok_all[ry, k, :, :, :, width:].reshape(group, LANES).astype(F32)
+        scale = jnp.sum(jnp.where(group_lane % experts == me, aux_rows, 0.0), axis=1, keepdims=True)
+
+        def step(j, comb):
+            cols = pl.ds(pl.multiple_of(j * TILE, TILE), TILE)
+            tok = tok_all[ry, k, :, :, :, :width].reshape(group, width)
+            cot = cot_all[ry, k].reshape(group, width)
+            gate = dot(tok, gate_w[:, cols], NN)
+            up = dot(tok, up_w[:, cols], NN)
+            raw = dot(cot, down_t[:, cols], NN)
+            sigmoid = 1.0 / (1.0 + jnp.exp(-gate))
+            act = gate * sigmoid
+            slope = sigmoid * (1.0 + gate * (1.0 - sigmoid))
+            hidden = act * up
+            grad = raw * scale
+            hid[at, :, cols] = (hidden * scale).astype(BF16)
+            gpart[at, :, cols] = (grad * up * slope).astype(BF16)
+            upart[at, :, cols] = (grad * act).astype(BF16)
+            return comb + jnp.sum(hidden * raw, axis=1, keepdims=True)
+
+        return lax.fori_loop(0, inner // TILE, step, jnp.zeros((group, 1), F32))
+
+    def terms(k, comb):
+        high, mid, low = split3(comb)
+        columns = jnp.where(
+            group_lane == me, high,
+            jnp.where(group_lane == me + experts, mid,
+                      jnp.where(group_lane == me + 2 * experts, low, 0.0)),
+        )
+        out_p[k, :, :, :, width:] = columns.astype(BF16).reshape(2, 2, rows, LANES)
+
+        def step(j, carry):
+            cols = pl.ds(pl.multiple_of(j * TILE, TILE), TILE)
+            out = dot(hid[k], down_w[:, cols], NN)
+            out_p[k, :, :, :, cols] = out.astype(BF16).reshape(2, 2, rows, TILE)
+            into = dot(gpart[k], gate_t[:, cols], NN) + dot(upart[k], up_t[:, cols], NN)
+            in_p[k, :, :, :, cols] = into.astype(BF16).reshape(2, 2, rows, TILE)
+            return carry
+
+        lax.fori_loop(0, width // TILE, step, 0)
+
+    partial = ((out_p, core_o, x_o, z_o), (in_p, core_i, x_i, z_i))
+
+    def sum_core_send(k):
+        for h, (p, c, _, _) in enumerate(partial):
+            copy(p.at[k, 1], c.at[k], device(rc=1), ("rc", k, h), ("rc", k, h))
+
+    def sum_core(k):
+        for h, (p, c, _, _) in enumerate(partial):
+            arrived(c.at[k], "rc", k, h)
+            p[k, 0] = (p[k, 0].astype(F32) + c[k].astype(F32)).astype(BF16)
+
+    def sum_x_send(k):
+        for h, (p, _, r, _) in enumerate(partial):
+            copy(p.at[k, 0, 1], r.at[k], device(rx=1), ("rx", k, h), ("rx", k, h))
+
+    def sum_x(k):
+        for h, (p, _, r, q) in enumerate(partial):
+            arrived(r.at[k], "rx", k, h)
+            p[k, 0, 0] = (p[k, 0, 0].astype(F32) + r[k].astype(F32)).astype(BF16)
+            copy(p.at[k, 0, 0], q.at[k - 1], device(rz=k), ("rz", k, h), ("rz", k, h))
+
+    def sum_last(h):
+        p, _, r, q = partial[h]
+        arrived(r.at[0], "rx", 0, h)
+        total = p[0, 0, 0].astype(F32) + r[0].astype(F32)
+        for k in range(1, 4):
+            arrived(q.at[k - 1], "rz", k, h)
+            total = total + q[k - 1].astype(F32)
+        return total
+
+    def weight_grads(spans, begin, end):
+        def d_step(j, carry):
+            at = pl.ds(pl.multiple_of(j * TILE, TILE), TILE)
+            cols = pl.ds(pl.multiple_of(dp * half + j * TILE, TILE), TILE)
+            for part, acc, ref in ((gpart, acc_g, gg_ref), (upart, acc_u, ug_ref)):
+                total = None
+                for ry, lo, hi in spans:
+                    n = (hi - lo) * group
+                    term = dot(
+                        tok_all[ry, lo:hi, :, :, :, cols].reshape(n, TILE),
+                        part[ry * 4 + lo : ry * 4 + hi].reshape(n, inner), TN,
+                    )
+                    total = term if total is None else total + term
+                if not begin:
+                    total = total + acc[at, :]
+                if end:
+                    ref[at, :] = total.astype(BF16)
+                else:
+                    acc[at, :] = total
+            return carry
+
+        lax.fori_loop(0, half // TILE, d_step, 0)
+
+        def f_step(j, carry):
+            at = pl.ds(pl.multiple_of(j * TILE, TILE), TILE)
+            cols = pl.ds(pl.multiple_of(dp * half, TILE), half)
+            total = None
+            for ry, lo, hi in spans:
+                n = (hi - lo) * group
+                term = dot(
+                    hid[ry * 4 + lo : ry * 4 + hi, :, at].reshape(n, TILE),
+                    cot_all[ry, lo:hi, :, :, :, cols].reshape(n, half), TN,
+                )
+                total = term if total is None else total + term
+            if not begin:
+                total = total + acc_d[at, :]
+            if end:
+                dg_ref[at, :] = total.astype(BF16)
+            else:
+                acc_d[at, :] = total
+            return carry
+
+        lax.fori_loop(0, inner // TILE, f_step, 0)
+
+    def flip(src, dst):
+        depth = src.shape[1]
+
+        def step(j, carry):
+            at = pl.ds(pl.multiple_of(j * TILE, TILE), TILE)
+            if src.shape[0] > depth:
+                dst[:, at] = src[at, :].T
+            else:
+                dst[at, :] = src[:, at].T
+            return carry
+
+        lax.fori_loop(0, max(src.shape) // TILE, step, 0)
+
+    for h in range(2):
+        z_send(h, 0, 1, 1)
+        later.append((h, 0, 1, 1, True))
+        middle_only((h, 0, 3, 3))
+        spread(0, h)
+    for load, src, dst in zip(loads, (down_w, gate_w, up_w), (down_t, gate_t, up_t)):
+        load.wait()
+        flip(src, dst)
+    for h in range(2):
+        on_z(1, h)
+    for h in range(2):
+        on_x(0, h)
+    on_core(0, 0)
+    terms(0, backprop(0, 0))
+    sum_core_send(0)
+    for h in range(2):
+        on_z(2, h)
+    for h in range(2):
+        on_x(1, h)
+    on_core(0, 1)
+    terms(1, backprop(0, 1))
+    sum_core_send(1)
+    sum_core(0)
+    for h in range(2):
+        on_z(3, h)
+    for h in range(2):
+        on_x(2, h)
+    on_core(0, 2)
+    terms(2, backprop(0, 2))
+    sum_core_send(2)
+    sum_core(1)
+    sum_x_send(1)
+    for h in range(2):
+        on_x(3, h)
+    on_core(0, 3)
+    terms(3, backprop(0, 3))
+    sum_core_send(3)
+    sum_core(2)
+    sum_x_send(2)
+    on_y(0)
+    on_core(1, 0)
+    backprop(1, 0)
+    sum_core(3)
+    sum_x_send(3)
+    sum_x_send(0)
+    sum_x(1)
+    on_y(1)
+    on_core(1, 1)
+    backprop(1, 1)
+    sum_x(2)
+    weight_grads(((0, 0, 4), (1, 0, 2)), True, False)
+    sum_x(3)
+    on_y(2)
+    on_core(1, 2)
+    backprop(1, 2)
+
+    total = sum_last(0)
+    out_ref[...] = total[:, :width].astype(BF16)
+    comb = total[:, width:]
+    comb = comb + pltpu.roll(comb, LANES - experts, 1) + pltpu.roll(comb, LANES - 2 * experts, 1)
+    comb = jnp.where(first, comb, 0.0)
+    probability, chosen, combine, sel_total = small[0], small[1], small[2], small[3]
+    mean = jnp.sum(combine * comb, axis=1, keepdims=True)
+    sel_grad = jnp.where(first, chosen * (comb - mean) / sel_total, 0.0)
+    logit_grad = probability * (sel_grad - jnp.sum(probability * sel_grad, axis=1, keepdims=True))
+    high, mid, low = split3(jnp.where(first, logit_grad, 0.0))
+    mine = (high + pltpu.roll(mid, experts, 1) + pltpu.roll(low, 2 * experts, 1)).astype(BF16)
+    lgs[0] = mine
+    for at, rel in enumerate(others):
+        pltpu.make_async_remote_copy(
+            src_ref=lgs.at[0], dst_ref=lgs.at[at + 1], send_sem=lg_send.at[at], recv_sem=lg_recv.at[at],
+            device_id=device(*rel), device_id_type=MESH,
+        ).start()
+    tgrad_ref[...] = (sum_last(1) + dot(mine, router_ref[...], NT)).astype(BF16)
+
+    on_y(3)
+    on_core(1, 3)
+    backprop(1, 3)
+    weight_grads(((1, 2, 4),), False, True)
+
+    for at, rel in enumerate(others):
+        pltpu.make_async_remote_copy(
+            src_ref=lgs.at[0], dst_ref=lgs.at[at + 1], send_sem=lg_send.at[at], recv_sem=lg_recv.at[at],
+            device_id=device(*rel), device_id_type=MESH,
+        ).wait()
+
+    def r_step(j, carry):
+        cols = pl.ds(pl.multiple_of(j * TILE, TILE), TILE)
+        total = None
+        for ry in range(2):
+            term = dot(
+                lgs[16 * ry : 16 * ry + 16].reshape(16 * rows, LANES),
+                tok_all[ry, :, :, :, :, cols].reshape(16 * rows, TILE), TN,
+            )
+            total = term if total is None else total + term
+        rgrad_ref[:, cols] = (
+            total[:experts] + total[experts : 2 * experts] + total[2 * experts : 3 * experts]
+        )
+        return carry
+
+    lax.fori_loop(0, width // TILE, r_step, 0)
+
+    for made in sent:
+        made.wait_send()
+
+    def z_done(h, from_rel, to_rel, land):
+        a = blocks[h]
+        pltpu.make_async_remote_copy(
+            src_ref=a.at[0, from_rel, 0, 0], dst_ref=a.at[0, land, 0, 0],
+            send_sem=send_sem.at[book("s", "z", from_rel, to_rel, h)],
+            recv_sem=recv_sem.at[book("z", land, h)],
+            device_id=device(rz=to_rel), device_id_type=MESH,
+        ).wait_send()
+
+    for args in later:
+        if len(args) == 5:
+            z_done(*args[:4])
+
+    @pl.when(middle_chip)
+    def _():
+        for args in later:
+            if len(args) == 4:
+                z_done(*args)
+
+    assert len(book.places) <= send_sem.shape[0]
+
+
+def local_fused(tokens, routes, cotangent, router_weight, gate_weight, up_weight, down_weight):
+    rows, width = tokens.shape
+    experts = router_weight.shape[1]
+    inner = gate_weight.shape[2]
+    half = width // 2
+    wide = width + LANES
+    vmem = lambda *shape, dtype=BF16: pltpu.VMEM(shape, dtype)
+    scratch = [
+        vmem(2, 4, 2, 2, rows, wide), vmem(2, 4, 2, 2, rows, width),
+        vmem(width, inner), vmem(width, inner), vmem(inner, width),
+        vmem(inner, width), vmem(inner, width), vmem(width, inner),
+        vmem(8, 4 * rows, inner), vmem(8, 4 * rows, inner), vmem(8, 4 * rows, inner),
+        vmem(4, 2, 2, rows, wide), vmem(4, 2, 2, rows, width),
+        vmem(4, 2, rows, wide), vmem(4, 2, rows, width),
+        vmem(4, rows, wide), vmem(4, rows, width),
+        vmem(3, rows, wide), vmem(3, rows, width),
+        vmem(32, rows, LANES),
+        vmem(half, inner, dtype=F32), vmem(half, inner, dtype=F32), vmem(inner, half, dtype=F32),
+        vmem(4, rows, LANES, dtype=F32),
+        pltpu.SemaphoreType.DMA((3,)),
+        pltpu.SemaphoreType.DMA((2 * COPIES,)), pltpu.SemaphoreType.DMA((2 * COPIES,)),
+        pltpu.SemaphoreType.DMA((31,)), pltpu.SemaphoreType.DMA((31,)),
+    ]
+    in_vmem = pl.BlockSpec(memory_space=pltpu.VMEM)
+    in_any = pl.BlockSpec(memory_space=pl.ANY)
+    layer_out, token_grad, gate_grad, up_grad, down_grad, router_grad = pl.pallas_call(
+        functools.partial(fused, experts),
+        out_shape=(
+            jax.ShapeDtypeStruct((rows, width), BF16),
+            jax.ShapeDtypeStruct((rows, width), BF16),
+            jax.ShapeDtypeStruct((half, inner), BF16),
+            jax.ShapeDtypeStruct((half, inner), BF16),
+            jax.ShapeDtypeStruct((inner, half), BF16),
+            jax.ShapeDtypeStruct((experts, width), F32),
+        ),
+        in_specs=[in_vmem] * 4 + [in_any] * 3,
+        out_specs=(in_vmem,) * 6,
+        scratch_shapes=scratch,
+        compiler_params=pltpu.CompilerParams(
+            collective_id=0, has_side_effects=True, vmem_limit_bytes=62 * 2**20
+        ),
+    )(
+        tokens, routes, cotangent, jnp.tile(router_weight, (1, LANES // experts)),
+        gate_weight[0], up_weight[0], down_weight[0],
+    )
+    return (
+        layer_out, token_grad, gate_grad[None], up_grad[None], down_grad[None], router_grad.T
+    )
 
 
 def silu_parts(gate_act):
@@ -128,138 +634,17 @@
     return (layer_out, token_grad, gate_grad, up_grad, down_grad, router_grad)
 
 
-def swap(array, bit):
-    if bit == 0:
-        return lax.ppermute(array, "dp", [(0, 1), (1, 0)])
-    size = lax.axis_size("expert")
-    return lax.ppermute(array, "expert", [(i, i ^ bit) for i in range(size)])
-
-
-def local_dense(tokens, routes, cotangent, router_weight, gate_weight, up_weight, down_weight):
-    tok_rows = tokens.shape[0]
-    model_width = tokens.shape[1]
-    expert_count = router_weight.shape[1]
-    group_size = lax.axis_size("expert")
-    dp_size = lax.axis_size("dp")
-    dp_index = lax.axis_index("dp")
-    expert_index = lax.axis_index("expert")
-    gate_mat, up_mat, down_mat = gate_weight[0], up_weight[0], down_weight[0]
-    logits = jnp.dot(tokens, router_weight, preferred_element_type=jnp.float32)
-    exp_logits = jnp.exp(logits)
-    probability = exp_logits / jnp.sum(exp_logits, axis=1, keepdims=True)
-    chosen = jnp.sum(
-        (routes[:, :, None] == jnp.arange(expert_count, dtype=jnp.int32)[None, None, :]).astype(
-            jnp.float32
-        ),
-        axis=1,
-    )
-    selected = chosen * probability
-    sel_total = jnp.sum(selected, axis=1, keepdims=True)
-    combine = selected / sel_total
-    bits = [1, 0, 2, 8, 4]
-    ones = (1,) * len(bits)
-
-    def gather(array, order):
-        array = array.reshape(ones + array.shape)
-        for bit in order:
-            array = jnp.concatenate([array, swap(array, bit)], axis=bits.index(bit))
-        return array.reshape((-1, array.shape[-1]))
-
-    combine_all = gather(combine, (4, 8, 2, 0, 1))
-    tokens_all = gather(tokens, (4, 8, 2, 0, 1))
-    cot_all = gather(cotangent, (4, 8, 0, 2, 1))
-    mine = (jnp.arange(expert_count, dtype=jnp.int32) == expert_index).astype(jnp.float32)
-    scale = jnp.sum(combine_all * mine[None, :], axis=1, keepdims=True)
-    gate_act = jnp.dot(tokens_all, gate_mat, preferred_element_type=jnp.float32)
-    up_act = jnp.dot(tokens_all, up_mat, preferred_element_type=jnp.float32)
-    raw_grad = lax.dot_general(
-        cot_all, down_mat, (((1,), (1,)), ((), ())), preferred_element_type=jnp.float32
-    )
-    act_value, act_slope = silu_parts(gate_act)
-    hidden = act_value * up_act
-    comb_mine = jnp.sum(hidden * raw_grad, axis=1)
-    scaled_hidden = (hidden * scale).astype(jnp.bfloat16)
-    hidden_grad = raw_grad * scale
-    gate_part = (hidden_grad * up_act * act_slope).astype(jnp.bfloat16)
-    up_part = (hidden_grad * act_value).astype(jnp.bfloat16)
-
-    def rows_of(array):
-        quarter = array.reshape((2, 2, group_size * tok_rows // 2) + array.shape[1:])
-        return quarter[:, 0].reshape((group_size * tok_rows,) + array.shape[1:])
-
-    def scatter(term):
-        term = term.reshape((2, 2, 2, 2, tok_rows, model_width))
-        for bit in (1, 2, 8, 4):
-            total = term[0].astype(jnp.float32) + swap(term[1], bit).astype(jnp.float32)
-            term = total.astype(jnp.bfloat16)
-        return total
-
-    out_term = jnp.dot(
-        rows_of(scaled_hidden), down_mat, preferred_element_type=jnp.float32
-    ).astype(jnp.bfloat16)
-    in_term = (
-        lax.dot_general(
-            rows_of(gate_part), gate_mat, (((1,), (1,)), ((), ())),
-            preferred_element_type=jnp.float32,
-        )
-        + lax.dot_general(
-            rows_of(up_part), up_mat, (((1,), (1,)), ((), ())),
-            preferred_element_type=jnp.float32,
-        )
-    ).astype(jnp.bfloat16)
-    layer_out = scatter(out_term).astype(jnp.bfloat16)
-    in_sum = scatter(in_term)
-    part_width = model_width // dp_size
-    start = dp_index * part_width
-    tokens_part = lax.dynamic_slice_in_dim(tokens_all, start, part_width, axis=1)
-    cot_part = lax.dynamic_slice_in_dim(cot_all, start, part_width, axis=1)
-    over_rows = (((0,), (0,)), ((), ()))
-    gate_grad = lax.dot_general(
-        tokens_part, gate_part, over_rows, preferred_element_type=jnp.float32
-    ).astype(jnp.bfloat16)
-    up_grad = lax.dot_general(
-        tokens_part, up_part, over_rows, preferred_element_type=jnp.float32
-    ).astype(jnp.bfloat16)
-    down_grad = lax.dot_general(
-        scaled_hidden, cot_part, over_rows, preferred_element_type=jnp.float32
-    ).astype(jnp.bfloat16)
-    comb = rows_of(comb_mine).reshape((2, 2, 2, 2, tok_rows, 1))
-    places = []
-    for step, bit in enumerate((1, 2, 8, 4)):
-        comb = jnp.concatenate([comb[0], swap(comb[1], bit)], axis=-1)
-        places = places + [p + bit for p in places] if step else [0, bit]
-    columns = jnp.asarray(places, jnp.int32) ^ expert_index
-    spread = (
-        columns[:, None] == jnp.arange(expert_count, dtype=jnp.int32)[None, :]
-    ).astype(jnp.float32)
-    comb_grad = jnp.sum(comb[:, :, None] * spread[None], axis=1)
-    sel_grad = (
-        chosen * (comb_grad - jnp.sum(combine * comb_grad, axis=1, keepdims=True)) / sel_total
-    )
-    logit_grad = probability * (sel_grad - jnp.sum(probability * sel_grad, axis=1, keepdims=True))
-    router_term = jnp.einsum(
-        "td,te->de", tokens.astype(jnp.float32), logit_grad, precision=lax.Precision.HIGHEST
-    )
-    router_grad = router_term
-    for bit in (1, 2, 0, 8, 4):
-        router_grad = router_grad + swap(router_grad, bit)
-    router_back = jnp.einsum(
-        "te,de->td", logit_grad, router_weight.astype(jnp.float32), precision=lax.Precision.HIGHEST
-    )
-    token_grad = (in_sum + router_back).astype(jnp.bfloat16)
-    return (layer_out, token_grad, gate_grad[None], up_grad[None], down_grad[None], router_grad)
-
-
 def local(tokens, routes, cotangent, router_weight, gate_weight, up_weight, down_weight):
     tok_rows, top_count = routes.shape
     capacity = min(tok_rows, 2 * tok_rows * top_count // router_weight.shape[1])
     dense = (
         capacity == tok_rows
         and gate_weight.shape[0] == 1
+        and router_weight.shape[1] == 16
         and lax.axis_size("dp") == 2
         and lax.axis_size("expert") == 16
     )
-    plan = local_dense if dense else local_slots
+    plan = local_fused if dense else local_slots
     return plan(tokens, routes, cotangent, router_weight, gate_weight, up_weight, down_weight)
 
 

time: 215 us -> 108 us (0.50)
  waiting for transfers between devices: 102 us -> 0 us
  Pallas kernels: 0 us -> 93.9 us
  starting transfers between devices: 55.2 us -> 0 us
  matrix products: 31.4 us -> 0 us
  other arithmetic: 19.1 us -> 0 us
  local copies, waits for them, and re-layouts: 4.47 us -> 12.9 us
    ppermute x32 -> x0, waiting for transfers between devices: 102 us -> none  [the longest x28 93.6 us: swap(): return lax.ppermute(array, 'expert', [(i, i ^ bit) for i in range(size)])]
    pallas_call x0 -> x1, Pallas kernels: none -> 93.9 us  [local_fused(): pl.pallas_call(functools.partial(fused, experts), out_shape=(jax.ShapeDty...]
    ppermute x32 -> x0, starting transfers between devices: 55.2 us -> none  [the longest x28 52.2 us: swap(): return lax.ppermute(array, 'expert', [(i, i ^ bit) for i in range(size)])]
    dot_general x12 -> x0, matrix products: 31.4 us -> none  [the longest x1 6.54 us: local_dense(): lax.dot_general(cot_all, down_mat, (((1,), (1,)), ((), ())), preferred_el...]
    concatenate x15 -> x0, other arithmetic: 13.4 us -> none  [the longest x14 13.4 us: gather(): array = jnp.concatenate([array, swap(array, bit)], axis=bits.index(bit))]
    unnamed x82 -> x13, local copies, waits for them, and re-layouts: 1.67 us -> 11.1 us
  transfers between devices with their start and end apart: 32 -> 0, of which waited for: 18 -> 0; matrix products, arithmetic and copies ran while one was open for 19% -> 0% of each run, Pallas kernels for 0% -> 0%
where the time goes in v1:
time: 108 us
  Pallas kernels  93.9 us (87%)
  local copies, waits for them, and re-layouts  12.9 us (12%)
    pallas_call x1, Pallas kernels, local_fused(): pl.pallas_call(functools.partial(fused, experts), out_shape=(jax.ShapeDty...  93.9 us
    unnamed x13, local copies, waits for them, and re-layouts  11.1 us

profile of v1, /device:TPU:1, one launch (start us, length us, event | category | flops | bytes accessed | tf_op | source)
XLA Modules:
  0.0 107.5 jit_solution(6370495363415240011)
XLA Ops:
  0.6 1.4 %copy.15.routes_ref = s32[32,8]{1,0:T(8,128)} copy(s32[32,8]{0,1:T(8,128)} %param.8) | data formatting | bytes 2048 | tf_op args[1]
  2.0 0.9 tile.4
  2.9 1.0 copy.16.router_ref
  3.9 93.9 %shard_map.118 = (bf16[32,2048]{1,0:T(8,128)(2,1)}, bf16[32,2048]{1,0:T(8,128)(2,1)}, bf16[1024,768]{1,0:T(8,128)(2,1)}, bf16[1024,768]{1,0:T(8,128)(2,1)}, bf16...) custom-call(bf16[32,2048]{1,0:T(8,128)(2,1)} %tok_ref.1, s32[32,8]{1,0:T(8,128)} %copy.15.routes_ref, bf16[32,2048]{1,0:T(8,128)(2,1)} %cot_ref.1, ...), custom_call_target="tpu_custom_call" | custom-call | tf_op jit(solution)/shard_map/pallas_call | solution.py:488
  97.8 1.6 %copy.23 = bf16[32,2048]{1,0:T(8,128)(2,1)} copy(bf16[32,2048]{1,0:T(8,128)(2,1)} %get-tuple-element.24) | data formatting | bytes 262144
  99.4 1.6 %copy.24 = bf16[32,2048]{1,0:T(8,128)(2,1)} copy(bf16[32,2048]{1,0:T(8,128)(2,1)} %get-tuple-element.25) | data formatting | bytes 262144
  101.0 0.0 copy-start.1
  101.0 2.8 %copy.25 = bf16[1,1024,768]{2,1,0:T(8,128)(2,1)} copy(bf16[1,1024,768]{2,1,0:T(8,128)(2,1)} %bitcast.14) | data formatting | bytes 3145728
  103.7 0.0 copy-done.1
  103.7 0.0 copy-start
  103.7 1.1 %copy.26 = bf16[1,1024,768]{2,1,0:T(8,128)(2,1)} copy(bf16[1,1024,768]{2,1,0:T(8,128)(2,1)S(1)} %bitcast.13) | data formatting | bytes 3145728
  104.9 0.8 copy-done
  105.7 0.0 copy-start.2
  105.7 1.1 %copy.27 = bf16[1,768,1024]{2,1,0:T(8,128)(2,1)} copy(bf16[1,768,1024]{2,1,0:T(8,128)(2,1)S(1)} %bitcast.12) | data formatting | bytes 3145728
  106.9 0.0 copy-done.2
  106.9 0.7 copy.28
Async XLA Ops:
  101.0 2.8 %copy-start.1 = (bf16[1024,768]{1,0:T(8,128)(2,1)S(1)}, bf16[1024,768]{1,0:T(8,128)(2,1)}, u32[]{:S(2)}) copy-start(bf16[1024,768]{1,0:T(8,128)(2,1)} %get-tuple-element.15) | copy-start | bytes 4718596
  103.7 2.0 %copy-start = (bf16[768,1024]{1,0:T(8,128)(2,1)S(1)}, bf16[768,1024]{1,0:T(8,128)(2,1)}, u32[]{:S(2)}) copy-start(bf16[768,1024]{1,0:T(8,128)(2,1)} %get-tuple-element.16) | copy-start | bytes 4718596
  105.7 1.1 %copy-start.2 = (f32[16,2048]{1,0:T(8,128)S(1)}, f32[16,2048]{1,0:T(8,128)}, u32[]{:S(2)}) copy-start(f32[16,2048]{1,0:T(8,128)} %get-tuple-element.17) | copy-start | bytes 393220

commit v2 on v1

--- a/solution.py
+++ b/solution.py
@@ -41,14 +41,16 @@
 
 def fused(
     experts, tok_ref, routes_ref, cot_ref, router_ref, gate_hbm, up_hbm, down_hbm,
-    out_ref, tgrad_ref, gg_ref, ug_ref, dg_ref, rgrad_ref,
+    out_ref, tgrad_ref, gg_hbm, ug_hbm, dg_hbm, rgrad_ref,
     tok_all, cot_all, gate_w, up_w, down_w, gate_t, up_t, down_t,
-    hid, gpart, upart, out_p, in_p, core_o, core_i, x_o, x_i, z_o, z_i,
-    lgs, acc_g, acc_u, acc_d, small, load_sem, send_sem, recv_sem, lg_send, lg_recv,
+    hid, gpart, upart, act_s, slope_s, hidden_s,
+    out_p, in_p, comb_p, core_o, core_i, core_c, x_o, x_i, x_c, z_o, z_i, z_c,
+    lgs, lgs_t, router_t, acc_g, acc_u, acc_d, gg_ref, ug_ref, dg_ref, small,
+    load_sem, store_sem, send_sem, recv_sem,
 ):
     rows, width = tok_ref.shape
     inner = gate_w.shape[1]
-    half = gg_ref.shape[0]
+    half = acc_g.shape[0]
     group = 4 * rows
     dp = lax.axis_index("dp")
     me = lax.axis_index("expert")
@@ -63,11 +65,9 @@
         )
 
     barrier = pltpu.get_barrier_semaphore()
-    others = [
-        (ry, rz, rc, rx) for ry in range(2) for rz in range(4) for rc in range(2) for rx in range(2)
-    ][1:]
-    for rel in others:
-        pl.semaphore_signal(barrier, inc=1, device_id=device(*rel), device_id_type=MESH)
+    others = [device(rc=1), device(rx=1), device(ry=1), device(rz=1), device(rz=2), device(rz=3)]
+    for other in others:
+        pl.semaphore_signal(barrier, inc=1, device_id=other, device_id_type=MESH)
 
     loads = [
         pltpu.make_async_copy(src, dst, load_sem.at[i])
@@ -77,14 +77,21 @@
         load.start()
 
     lane = lax.broadcasted_iota(jnp.int32, (rows, LANES), 1)
-    expert_lane = lane % experts
     first = lane < experts
-    exp_logits = jnp.exp(dot(tok_ref[...], router_ref[...], NN))
+    for i in range(LANES // experts):
+        router_t[i * experts : (i + 1) * experts, :] = router_ref[...]
+    exp_logits = jnp.exp(dot(tok_ref[...], router_t[...], NT))
     masked = jnp.where(first, exp_logits, 0.0)
     probability = exp_logits / jnp.sum(masked, axis=1, keepdims=True)
-    chosen = jnp.zeros((rows, LANES), F32)
-    for k in range(routes_ref.shape[1]):
-        chosen = chosen + (routes_ref[:, k : k + 1] == expert_lane).astype(F32)
+    chosen = jnp.zeros((LANES, rows), F32)
+    expert_row = lax.broadcasted_iota(jnp.int32, (LANES, rows), 0) % experts
+    for k in range(routes_ref.shape[0]):
+        chosen = chosen + (routes_ref[k : k + 1, :] == expert_row).astype(F32)
+    eye = (
+        lax.broadcasted_iota(jnp.int32, (rows, rows), 0)
+        == lax.broadcasted_iota(jnp.int32, (rows, rows), 1)
+    ).astype(F32)
+    chosen = dot(eye.astype(BF16), chosen.astype(BF16), NT)
     selected = chosen * probability
     sel_total = jnp.sum(jnp.where(first, selected, 0.0), axis=1, keepdims=True)
     combine = selected / sel_total
@@ -159,115 +166,127 @@
         to_y(k, 0, h)
 
     def on_z(k, h):
+        here = blocks[h]
         if k == 1:
-            arrived(blocks[h].at[0, 1, 0, 0], "z", 1, h)
-            middle_only((h, 1, 3, 2))
-            spread(1, h)
-        elif k == 2:
+            arrived(here.at[0, 1, 0, 0], "z", 1, h)
+
             @pl.when(middle_chip)
             def _():
-                arrived(blocks[h].at[0, 3, 0, 0], "z", 3, h)
+                z_send(h, 1, 3, 2)
+                arrived(here.at[0, 3, 0, 0], "z", 3, h)
                 z_send(h, 3, 1, 2)
-                arrived(blocks[h].at[0, 2, 0, 0], "z", 2, h)
-                z_send(h, 2, 1, 3)
-
-            later.extend([(h, 3, 1, 2), (h, 2, 1, 3)])
+
+            later.extend([(h, 1, 3, 2), (h, 3, 1, 2)])
+        elif k == 2:
+            arrived(here.at[0, 2, 0, 0], "z", 2, h)
+            middle_only((h, 2, 1, 3))
+        else:
 
             @pl.when(jnp.logical_not(middle_chip))
             def _():
-                arrived(blocks[h].at[0, 2, 0, 0], "z", 2, h)
-
-            spread(2, h)
-        else:
-            @pl.when(jnp.logical_not(middle_chip))
-            def _():
-                arrived(blocks[h].at[0, 3, 0, 0], "z", 3, h)
-
-            spread(3, h)
+                arrived(here.at[0, 3, 0, 0], "z", 3, h)
+
+        spread(k, h)
 
     def on_x(k, h):
         arrived(blocks[h].at[0, k, 0, 1], "x", k, h)
         to_core(0, k, 1, h)
         to_y(k, 1, h)
 
-    def on_y(k):
-        for h in range(2):
-            for rx in range(2):
-                arrived(blocks[h].at[1, k, 0, rx], "y", k, rx, h)
-                to_core(1, k, rx, h)
-
-    def on_core(ry, k):
-        for h in range(2):
-            for rx in range(2):
-                arrived(blocks[h].at[ry, k, 1, rx], "c", ry, k, rx, h)
+    def on_y(k, h):
+        for rx in range(2):
+            arrived(blocks[h].at[1, k, 0, rx], "y", k, rx, h)
+            to_core(1, k, rx, h)
+
+    def on_core(ry, k, h):
+        for rx in range(2):
+            arrived(blocks[h].at[ry, k, 1, rx], "c", ry, k, rx, h)
 
     group_lane = lax.broadcasted_iota(jnp.int32, (group, LANES), 1)
 
-    def backprop(ry, k):
-        at = ry * 4 + k
+    def scale_of(ry, k):
         aux_rows = tok_all[ry, k, :, :, :, width:].reshape(group, LANES).astype(F32)
-        scale = jnp.sum(jnp.where(group_lane % experts == me, aux_rows, 0.0), axis=1, keepdims=True)
+        return jnp.sum(jnp.where(group_lane % experts == me, aux_rows, 0.0), axis=1, keepdims=True)
+
+    def forward(ry, k):
+        scale = scale_of(ry, k)
+
+        def step(j, carry):
+            cols = pl.ds(pl.multiple_of(j * TILE, TILE), TILE)
+            tok = tok_all[ry, k, :, :, :, :width].reshape(group, width)
+            gate = dot(tok, gate_w[:, cols], NN)
+            up = dot(tok, up_w[:, cols], NN)
+            sigmoid = 1.0 / (1.0 + jnp.exp(-gate))
+            act = gate * sigmoid
+            hidden = act * up
+            act_s[:, cols] = act
+            slope_s[:, cols] = up * (sigmoid * (1.0 + gate * (1.0 - sigmoid)))
+            hidden_s[:, cols] = hidden
+            hid[ry * 4 + k, :, cols] = (hidden * scale).astype(BF16)
+            return carry
+
+        lax.fori_loop(0, inner // TILE, step, 0, unroll=True)
+
+    def backward(ry, k):
+        scale = scale_of(ry, k)
 
         def step(j, comb):
             cols = pl.ds(pl.multiple_of(j * TILE, TILE), TILE)
-            tok = tok_all[ry, k, :, :, :, :width].reshape(group, width)
-            cot = cot_all[ry, k].reshape(group, width)
-            gate = dot(tok, gate_w[:, cols], NN)
-            up = dot(tok, up_w[:, cols], NN)
-            raw = dot(cot, down_t[:, cols], NN)
-            sigmoid = 1.0 / (1.0 + jnp.exp(-gate))
-            act = gate * sigmoid
-            slope = sigmoid * (1.0 + gate * (1.0 - sigmoid))
-            hidden = act * up
+            raw = dot(cot_all[ry, k].reshape(group, width), down_t[:, cols], NN)
             grad = raw * scale
-            hid[at, :, cols] = (hidden * scale).astype(BF16)
-            gpart[at, :, cols] = (grad * up * slope).astype(BF16)
-            upart[at, :, cols] = (grad * act).astype(BF16)
-            return comb + jnp.sum(hidden * raw, axis=1, keepdims=True)
-
-        return lax.fori_loop(0, inner // TILE, step, jnp.zeros((group, 1), F32))
-
-    def terms(k, comb):
-        high, mid, low = split3(comb)
-        columns = jnp.where(
-            group_lane == me, high,
-            jnp.where(group_lane == me + experts, mid,
-                      jnp.where(group_lane == me + 2 * experts, low, 0.0)),
-        )
-        out_p[k, :, :, :, width:] = columns.astype(BF16).reshape(2, 2, rows, LANES)
-
+            gpart[ry * 4 + k, :, cols] = (grad * slope_s[:, cols]).astype(BF16)
+            upart[ry * 4 + k, :, cols] = (grad * act_s[:, cols]).astype(BF16)
+            return comb + jnp.sum(hidden_s[:, cols] * raw, axis=1, keepdims=True)
+
+        comb = lax.fori_loop(0, inner // TILE, step, jnp.zeros((group, 1), F32), unroll=True)
+        if ry == 0:
+            high, mid, low = split3(comb)
+            columns = jnp.where(
+                group_lane == me, high,
+                jnp.where(group_lane == me + experts, mid,
+                          jnp.where(group_lane == me + 2 * experts, low, 0.0)),
+            )
+            comb_p[k] = columns.astype(BF16).reshape(2, 2, rows, LANES)
+
+    def out_terms(k):
         def step(j, carry):
             cols = pl.ds(pl.multiple_of(j * TILE, TILE), TILE)
             out = dot(hid[k], down_w[:, cols], NN)
             out_p[k, :, :, :, cols] = out.astype(BF16).reshape(2, 2, rows, TILE)
+            return carry
+
+        lax.fori_loop(0, width // TILE, step, 0, unroll=True)
+        core_send(k, 0)
+
+    def in_terms(k):
+        def step(j, carry):
+            cols = pl.ds(pl.multiple_of(j * TILE, TILE), TILE)
             into = dot(gpart[k], gate_t[:, cols], NN) + dot(upart[k], up_t[:, cols], NN)
             in_p[k, :, :, :, cols] = into.astype(BF16).reshape(2, 2, rows, TILE)
             return carry
 
-        lax.fori_loop(0, width // TILE, step, 0)
+        lax.fori_loop(0, width // TILE, step, 0, unroll=True)
+        core_send(k, 1)
 
     partial = ((out_p, core_o, x_o, z_o), (in_p, core_i, x_i, z_i))
 
-    def sum_core_send(k):
-        for h, (p, c, _, _) in enumerate(partial):
-            copy(p.at[k, 1], c.at[k], device(rc=1), ("rc", k, h), ("rc", k, h))
-
-    def sum_core(k):
-        for h, (p, c, _, _) in enumerate(partial):
-            arrived(c.at[k], "rc", k, h)
-            p[k, 0] = (p[k, 0].astype(F32) + c[k].astype(F32)).astype(BF16)
-
-    def sum_x_send(k):
-        for h, (p, _, r, _) in enumerate(partial):
-            copy(p.at[k, 0, 1], r.at[k], device(rx=1), ("rx", k, h), ("rx", k, h))
-
-    def sum_x(k):
-        for h, (p, _, r, q) in enumerate(partial):
-            arrived(r.at[k], "rx", k, h)
-            p[k, 0, 0] = (p[k, 0, 0].astype(F32) + r[k].astype(F32)).astype(BF16)
-            copy(p.at[k, 0, 0], q.at[k - 1], device(rz=k), ("rz", k, h), ("rz", k, h))
-
-    def sum_last(h):
+    def core_send(k, h):
+        p, c, _, _ = partial[h]
+        copy(p.at[k, 1], c.at[k], device(rc=1), ("rc", k, h), ("rc", k, h))
+
+    def core_sum(k, h):
+        p, c, r, _ = partial[h]
+        arrived(c.at[k], "rc", k, h)
+        p[k, 0] = (p[k, 0].astype(F32) + c[k].astype(F32)).astype(BF16)
+        copy(p.at[k, 0, 1], r.at[k], device(rx=1), ("rx", k, h), ("rx", k, h))
+
+    def x_sum(k, h):
+        p, _, r, q = partial[h]
+        arrived(r.at[k], "rx", k, h)
+        p[k, 0, 0] = (p[k, 0, 0].astype(F32) + r[k].astype(F32)).astype(BF16)
+        copy(p.at[k, 0, 0], q.at[k - 1], device(rz=k), ("rz", k, h), ("rz", k, h))
+
+    def last_sum(h):
         p, _, r, q = partial[h]
         arrived(r.at[0], "rx", 0, h)
         total = p[0, 0, 0].astype(F32) + r[0].astype(F32)
@@ -276,7 +295,28 @@
             total = total + q[k - 1].astype(F32)
         return total
 
-    def weight_grads(spans, begin, end):
+    def comb_send():
+        copy(comb_p.at[:, 1], core_c, device(rc=1), ("cc",), ("cc",))
+
+    def comb_core():
+        arrived(core_c, "cc")
+        comb_p[:, 0] = (comb_p[:, 0].astype(F32) + core_c[...].astype(F32)).astype(BF16)
+        copy(comb_p.at[:, 0, 1], x_c, device(rx=1), ("cx",), ("cx",))
+
+    def comb_x():
+        arrived(x_c, "cx")
+        comb_p[:, 0, 0] = (comb_p[:, 0, 0].astype(F32) + x_c[...].astype(F32)).astype(BF16)
+        for k in range(1, 4):
+            copy(comb_p.at[k, 0, 0], z_c.at[k - 1], device(rz=k), ("cz", k), ("cz", k))
+
+    def comb_last():
+        total = comb_p[0, 0, 0].astype(F32)
+        for k in range(1, 4):
+            arrived(z_c.at[k - 1], "cz", k)
+            total = total + z_c[k - 1].astype(F32)
+        return total
+
+    def width_grads(spans, begin, end):
         def d_step(j, carry):
             at = pl.ds(pl.multiple_of(j * TILE, TILE), TILE)
             cols = pl.ds(pl.multiple_of(dp * half + j * TILE, TILE), TILE)
@@ -297,8 +337,9 @@
                     acc[at, :] = total
             return carry
 
-        lax.fori_loop(0, half // TILE, d_step, 0)
-
+        lax.fori_loop(0, half // TILE, d_step, 0, unroll=True)
+
+    def inner_grads(spans, begin, end):
         def f_step(j, carry):
             at = pl.ds(pl.multiple_of(j * TILE, TILE), TILE)
             cols = pl.ds(pl.multiple_of(dp * half, TILE), half)
@@ -318,7 +359,7 @@
                 acc_d[at, :] = total
             return carry
 
-        lax.fori_loop(0, inner // TILE, f_step, 0)
+        lax.fori_loop(0, inner // TILE, f_step, 0, unroll=True)
 
     def flip(src, dst):
         depth = src.shape[1]
@@ -331,7 +372,7 @@
                 dst[at, :] = src[:, at].T
             return carry
 
-        lax.fori_loop(0, max(src.shape) // TILE, step, 0)
+        lax.fori_loop(0, max(src.shape) // TILE, step, 0, unroll=True)
 
     for h in range(2):
         z_send(h, 0, 1, 1)
@@ -341,57 +382,61 @@
     for load, src, dst in zip(loads, (down_w, gate_w, up_w), (down_t, gate_t, up_t)):
         load.wait()
         flip(src, dst)
-    for h in range(2):
-        on_z(1, h)
-    for h in range(2):
-        on_x(0, h)
-    on_core(0, 0)
-    terms(0, backprop(0, 0))
-    sum_core_send(0)
-    for h in range(2):
-        on_z(2, h)
-    for h in range(2):
-        on_x(1, h)
-    on_core(0, 1)
-    terms(1, backprop(0, 1))
-    sum_core_send(1)
-    sum_core(0)
-    for h in range(2):
-        on_z(3, h)
-    for h in range(2):
-        on_x(2, h)
-    on_core(0, 2)
-    terms(2, backprop(0, 2))
-    sum_core_send(2)
-    sum_core(1)
-    sum_x_send(1)
-    for h in range(2):
-        on_x(3, h)
-    on_core(0, 3)
-    terms(3, backprop(0, 3))
-    sum_core_send(3)
-    sum_core(2)
-    sum_x_send(2)
-    on_y(0)
-    on_core(1, 0)
-    backprop(1, 0)
-    sum_core(3)
-    sum_x_send(3)
-    sum_x_send(0)
-    sum_x(1)
-    on_y(1)
-    on_core(1, 1)
-    backprop(1, 1)
-    sum_x(2)
-    weight_grads(((0, 0, 4), (1, 0, 2)), True, False)
-    sum_x(3)
-    on_y(2)
-    on_core(1, 2)
-    backprop(1, 2)
-
-    total = sum_last(0)
-    out_ref[...] = total[:, :width].astype(BF16)
-    comb = total[:, width:]
+    TOK, COT, OUT, IN = 0, 1, 0, 1
+    for k in range(4):
+        for h in (TOK, COT):
+            if k < 3:
+                on_z(k + 1, h)
+            on_x(k, h)
+            on_core(0, k, h)
+            if h == TOK:
+                forward(0, k)
+                if k == 3:
+                    core_sum(2, IN)
+                out_terms(k)
+            else:
+                backward(0, k)
+                if k == 2:
+                    core_sum(2, OUT)
+                if k == 3:
+                    core_sum(3, OUT)
+                    x_sum(2, OUT)
+                in_terms(k)
+    comb_send()
+    for h in (TOK, COT):
+        on_y(0, h)
+    core_sum(3, IN)
+    x_sum(3, OUT)
+    x_sum(2, IN)
+    comb_core()
+    core_sum(1, OUT)
+    core_sum(1, IN)
+    core_sum(0, OUT)
+    core_sum(0, IN)
+    on_core(1, 0, TOK)
+    forward(1, 0)
+    on_core(1, 0, COT)
+    backward(1, 0)
+    comb_x()
+    x_sum(3, IN)
+    for h in (TOK, COT):
+        on_y(1, h)
+    on_core(1, 1, TOK)
+    forward(1, 1)
+    on_core(1, 1, COT)
+    backward(1, 1)
+    width_grads(((0, 0, 4), (1, 0, 2)), True, False)
+    x_sum(1, OUT)
+    x_sum(1, IN)
+    inner_grads(((0, 0, 4), (1, 0, 2)), True, False)
+    for h in (TOK, COT):
+        on_y(2, h)
+    on_core(1, 2, TOK)
+    forward(1, 2)
+    on_core(1, 2, COT)
+    backward(1, 2)
+
+    comb = comb_last()
     comb = comb + pltpu.roll(comb, LANES - experts, 1) + pltpu.roll(comb, LANES - 2 * experts, 1)
     comb = jnp.where(first, comb, 0.0)
     probability, chosen, combine, sel_total = small[0], small[1], small[2], small[3]
@@ -400,41 +445,66 @@
     logit_grad = probability * (sel_grad - jnp.sum(probability * sel_grad, axis=1, keepdims=True))
     high, mid, low = split3(jnp.where(first, logit_grad, 0.0))
     mine = (high + pltpu.roll(mid, experts, 1) + pltpu.roll(low, 2 * experts, 1)).astype(BF16)
-    lgs[0] = mine
-    for at, rel in enumerate(others):
-        pltpu.make_async_remote_copy(
-            src_ref=lgs.at[0], dst_ref=lgs.at[at + 1], send_sem=lg_send.at[at], recv_sem=lg_recv.at[at],
-            device_id=device(*rel), device_id_type=MESH,
-        ).start()
-    tgrad_ref[...] = (sum_last(1) + dot(mine, router_ref[...], NT)).astype(BF16)
-
-    on_y(3)
-    on_core(1, 3)
-    backprop(1, 3)
-    weight_grads(((1, 2, 4),), False, True)
-
-    for at, rel in enumerate(others):
-        pltpu.make_async_remote_copy(
-            src_ref=lgs.at[0], dst_ref=lgs.at[at + 1], send_sem=lg_send.at[at], recv_sem=lg_recv.at[at],
-            device_id=device(*rel), device_id_type=MESH,
-        ).wait()
+    lgs[0, 0, 0, 0] = mine
+    hops = (
+        (lgs.at[0, 0, 0, 0], lgs.at[0, 0, 1, 0], device(rc=1)),
+        (lgs.at[0, 0, :, 0], lgs.at[0, 0, :, 1], device(rx=1)),
+        (lgs.at[0, 0], lgs.at[0, 1], device(rz=1)),
+        (lgs.at[0, 0], lgs.at[0, 2], device(rz=2)),
+        (lgs.at[0, 0], lgs.at[0, 3], device(rz=3)),
+        (lgs.at[0], lgs.at[1], device(ry=1)),
+    )
+
+    def hop(*steps):
+        for i in steps:
+            src, dst, to = hops[i]
+            copy(src, dst, to, ("l", i), ("l", i))
+
+    def hopped(*steps):
+        for i in steps:
+            arrived(hops[i][1], "l", i)
+
+    hop(0)
+    out_ref[...] = last_sum(OUT).astype(BF16)
+    on_y(3, TOK)
+    on_core(1, 3, TOK)
+    forward(1, 3)
+    hopped(0)
+    hop(1)
+    on_y(3, COT)
+    hopped(1)
+    hop(2, 3, 4)
+    on_core(1, 3, COT)
+    backward(1, 3)
+    stores = [
+        pltpu.make_async_copy(src, dst, store_sem.at[i])
+        for i, (src, dst) in enumerate(((gg_ref, gg_hbm), (ug_ref, ug_hbm), (dg_ref, dg_hbm)))
+    ]
+    width_grads(((1, 2, 4),), False, True)
+    stores[0].start()
+    stores[1].start()
+    hopped(2, 3, 4)
+    hop(5)
+    inner_grads(((1, 2, 4),), False, True)
+    stores[2].start()
+    tgrad_ref[...] = (last_sum(IN) + dot(mine, router_t[...], NN)).astype(BF16)
+    hopped(5)
+    lgs_t[...] = lgs[...].reshape(32 * rows, LANES).astype(F32).T.astype(BF16)
 
     def r_step(j, carry):
         cols = pl.ds(pl.multiple_of(j * TILE, TILE), TILE)
-        total = None
-        for ry in range(2):
-            term = dot(
-                lgs[16 * ry : 16 * ry + 16].reshape(16 * rows, LANES),
-                tok_all[ry, :, :, :, :, cols].reshape(16 * rows, TILE), TN,
-            )
-            total = term if total is None else total + term
+        total = dot(
+            lgs_t[: 3 * experts, :], tok_all[:, :, :, :, :, cols].reshape(32 * rows, TILE), NN
+        )
         rgrad_ref[:, cols] = (
             total[:experts] + total[experts : 2 * experts] + total[2 * experts : 3 * experts]
         )
         return carry
 
-    lax.fori_loop(0, width // TILE, r_step, 0)
-
+    lax.fori_loop(0, width // TILE, r_step, 0, unroll=True)
+
+    for store in stores:
+        store.wait()
     for made in sent:
         made.wait_send()
 
@@ -458,6 +528,39 @@
                 z_done(*args)
 
     assert len(book.places) <= send_sem.shape[0]
+
+
+def hand_over(arrays):
+    n = len(arrays)
+    pieces = [4 if a.shape[0] >= 128 else 2 for a in arrays]
+
+    def kernel(*refs):
+        sources, targets, held = refs[:n], refs[n : 2 * n], refs[2 * n : 3 * n]
+        in_sem, out_sem = refs[3 * n :]
+        ins, outs = [], []
+        for i in range(n):
+            step = arrays[i].shape[0] // pieces[i]
+            for j in range(pieces[i]):
+                at = pl.ds(j * step, step)
+                ins.append(pltpu.make_async_copy(sources[i].at[at], held[i].at[at], in_sem.at[i, j]))
+                outs.append(pltpu.make_async_copy(held[i].at[at], targets[i].at[at], out_sem.at[i, j]))
+        for made in ins:
+            made.start()
+        for before, made in zip(ins, outs):
+            before.wait()
+            made.start()
+        for made in outs:
+            made.wait()
+
+    return pl.pallas_call(
+        kernel,
+        out_shape=tuple(jax.ShapeDtypeStruct(a.shape, a.dtype) for a in arrays),
+        in_specs=[pl.BlockSpec(memory_space=pl.ANY)] * n,
+        out_specs=(pl.BlockSpec(memory_space=pl.ANY),) * n,
+        scratch_shapes=[pltpu.VMEM(a.shape, a.dtype) for a in arrays]
+        + [pltpu.SemaphoreType.DMA((n, 4)), pltpu.SemaphoreType.DMA((n, 4))],
+        compiler_params=pltpu.CompilerParams(vmem_limit_bytes=60 * 2**20),
+    )(*arrays)
 
 
 def local_fused(tokens, routes, cotangent, router_weight, gate_weight, up_weight, down_weight):
@@ -472,20 +575,22 @@
         vmem(width, inner), vmem(width, inner), vmem(inner, width),
         vmem(inner, width), vmem(inner, width), vmem(width, inner),
         vmem(8, 4 * rows, inner), vmem(8, 4 * rows, inner), vmem(8, 4 * rows, inner),
-        vmem(4, 2, 2, rows, wide), vmem(4, 2, 2, rows, width),
-        vmem(4, 2, rows, wide), vmem(4, 2, rows, width),
-        vmem(4, rows, wide), vmem(4, rows, width),
-        vmem(3, rows, wide), vmem(3, rows, width),
-        vmem(32, rows, LANES),
+        vmem(4 * rows, inner, dtype=F32), vmem(4 * rows, inner, dtype=F32),
+        vmem(4 * rows, inner, dtype=F32),
+        vmem(4, 2, 2, rows, width), vmem(4, 2, 2, rows, width), vmem(4, 2, 2, rows, LANES),
+        vmem(4, 2, rows, width), vmem(4, 2, rows, width), vmem(4, 2, rows, LANES),
+        vmem(4, rows, width), vmem(4, rows, width), vmem(4, rows, LANES),
+        vmem(3, rows, width), vmem(3, rows, width), vmem(3, rows, LANES),
+        vmem(2, 4, 2, 2, rows, LANES), vmem(LANES, 32 * rows), vmem(LANES, width),
         vmem(half, inner, dtype=F32), vmem(half, inner, dtype=F32), vmem(inner, half, dtype=F32),
+        vmem(half, inner), vmem(half, inner), vmem(inner, half),
         vmem(4, rows, LANES, dtype=F32),
-        pltpu.SemaphoreType.DMA((3,)),
+        pltpu.SemaphoreType.DMA((3,)), pltpu.SemaphoreType.DMA((3,)),
         pltpu.SemaphoreType.DMA((2 * COPIES,)), pltpu.SemaphoreType.DMA((2 * COPIES,)),
-        pltpu.SemaphoreType.DMA((31,)), pltpu.SemaphoreType.DMA((31,)),
     ]
     in_vmem = pl.BlockSpec(memory_space=pltpu.VMEM)
     in_any = pl.BlockSpec(memory_space=pl.ANY)
-    layer_out, token_grad, gate_grad, up_grad, down_grad, router_grad = pl.pallas_call(
+    results = pl.pallas_call(
         functools.partial(fused, experts),
         out_shape=(
             jax.ShapeDtypeStruct((rows, width), BF16),
@@ -496,15 +601,15 @@
             jax.ShapeDtypeStruct((experts, width), F32),
         ),
         in_specs=[in_vmem] * 4 + [in_any] * 3,
-        out_specs=(in_vmem,) * 6,
+        out_specs=(in_vmem, in_vmem, in_any, in_any, in_any, in_vmem),
         scratch_shapes=scratch,
         compiler_params=pltpu.CompilerParams(
             collective_id=0, has_side_effects=True, vmem_limit_bytes=62 * 2**20
         ),
     )(
-        tokens, routes, cotangent, jnp.tile(router_weight, (1, LANES // experts)),
-        gate_weight[0], up_weight[0], down_weight[0],
-    )
+        tokens, routes.T, cotangent, router_weight.T, gate_weight[0], up_weight[0], down_weight[0]
+    )
+    layer_out, token_grad, gate_grad, up_grad, down_grad, router_grad = hand_over(results)
     return (
         layer_out, token_grad, gate_grad[None], up_grad[None], down_grad[None], router_grad.T
     )

time: 108 us -> 87.6 us (0.81)
  local copies, waits for them, and re-layouts: 12.9 us -> 0 us
  Pallas kernels: 93.9 us -> 85.8 us
    pallas_call x1, Pallas kernels: 93.9 us -> 80.9 us  [local_fused(): pl.pallas_call(functools.partial(fused, experts), out_shape=(jax.ShapeDty...]
    unnamed x13 -> x0, local copies, waits for them, and re-layouts: 11.1 us -> none
    pallas_call x0 -> x1, Pallas kernels: none -> 4.91 us  [hand_over(): pl.pallas_call(kernel, out_shape=tuple((jax.ShapeDtypeStruct(a.shape, a.d...]
    another operation x2 -> x0, local copies, waits for them, and re-layouts: 1.88 us -> none  [local_fused(): jnp.tile(router_weight, (1, LANES // experts))]
where the time goes in v2:
time: 87.6 us; the launch traced here: 86.6 us
  Pallas kernels  85.8 us (98%)
    pallas_call x1, Pallas kernels, local_fused(): pl.pallas_call(functools.partial(fused, experts), out_shape=(jax.ShapeDty...  80.9 us
    pallas_call x1, Pallas kernels, hand_over(): pl.pallas_call(kernel, out_shape=tuple((jax.ShapeDtypeStruct(a.shape, a.d...  4.91 us

profile of v2, /device:TPU:1, one launch (start us, length us, event | category | flops | bytes accessed | tf_op | source)
XLA Modules:
  0.0 86.6 jit_solution(11754294263599624702)
XLA Ops:
  0.6 80.9 %shard_map.118 = (bf16[32,2048]{1,0:T(8,128)(2,1)}, bf16[32,2048]{1,0:T(8,128)(2,1)}, bf16[1024,768]{1,0:T(8,128)(2,1)}, bf16[1024,768]{1,0:T(8,128)(2,1)}, bf16...) custom-call(bf16[32,2048]{1,0:T(8,128)(2,1)} %tok_ref.1, s32[8,32]{1,0:T(8,128)} %bitcast.13, bf16[32,2048]{1,0:T(8,128)(2,1)} %cot_ref.1, ...), custom_call_target="tpu_custom_call" | custom-call | tf_op jit(solution)/shard_map/pallas_call | solution.py:593
  81.5 4.9 %shard_map.119 = (bf16[32,2048]{1,0:T(8,128)(2,1)}, bf16[32,2048]{1,0:T(8,128)(2,1)}, bf16[1024,768]{1,0:T(8,128)(2,1)}, bf16[1024,768]{1,0:T(8,128)(2,1)}, bf16...) custom-call(bf16[32,2048]{1,0:T(8,128)(2,1)} %get-tuple-element.18.refs_0_, bf16[32,2048]{1,0:T(8,128)(2,1)} %get-tuple-element.19.refs_1_, ...), custom_call_target="tpu_custom_call" | custom-call | tf_op jit(solution)/shard_map/pallas_call | solution.py:555

commit v3 on v2

--- a/solution.py
+++ b/solution.py
@@ -44,8 +44,8 @@
     out_ref, tgrad_ref, gg_hbm, ug_hbm, dg_hbm, rgrad_ref,
     tok_all, cot_all, gate_w, up_w, down_w, gate_t, up_t, down_t,
     hid, gpart, upart, act_s, slope_s, hidden_s,
-    out_p, in_p, comb_p, core_o, core_i, core_c, x_o, x_i, x_c, z_o, z_i, z_c,
-    lgs, lgs_t, router_t, acc_g, acc_u, acc_d, gg_ref, ug_ref, dg_ref, small,
+    out_p, in_p, core_o, core_i, x_o, x_i, z_o, z_i,
+    combs, comb_s, lgs_t, router_t, acc_g, acc_u, acc_d, gg_ref, ug_ref, dg_ref,
     load_sem, store_sem, send_sem, recv_sem,
 ):
     rows, width = tok_ref.shape
@@ -96,15 +96,12 @@
     sel_total = jnp.sum(jnp.where(first, selected, 0.0), axis=1, keepdims=True)
     combine = selected / sel_total
     part = lane // experts
-    high, mid, low = split3(combine)
-    aux = jnp.where(part == 0, high, jnp.where(part == 1, mid, jnp.where(part == 2, low, 0.0)))
+    aux = jnp.zeros((rows, LANES), F32)
+    for i, term in enumerate(split3(combine) + split3(probability)):
+        aux = jnp.where(part == i, term, aux)
     tok_all[0, 0, 0, 0, :, :width] = tok_ref[...]
     tok_all[0, 0, 0, 0, :, width:] = aux.astype(BF16)
     cot_all[0, 0, 0, 0] = cot_ref[...]
-    small[0] = probability
-    small[1] = chosen
-    small[2] = combine
-    small[3] = jnp.broadcast_to(sel_total, (rows, LANES))
 
     pl.semaphore_wait(barrier, len(others))
 
@@ -163,7 +160,8 @@
     def spread(k, h):
         to_x(k, h)
         to_core(0, k, 0, h)
-        to_y(k, 0, h)
+        if k != 1:
+            to_y(k, 0, h)
 
     def on_z(k, h):
         here = blocks[h]
@@ -193,10 +191,12 @@
         to_core(0, k, 1, h)
         to_y(k, 1, h)
 
-    def on_y(k, h):
-        for rx in range(2):
-            arrived(blocks[h].at[1, k, 0, rx], "y", k, rx, h)
-            to_core(1, k, rx, h)
+    def on_y(k, rx, h):
+        a = blocks[h]
+        arrived(a.at[1, k, 0, rx], "y", k, rx, h)
+        to_core(1, k, rx, h)
+        if (k, rx) == (0, 0):
+            copy(a.at[1, 0, 0, 0], a.at[1, 1, 0, 0], device(rz=1), ("yz", h), ("y", 1, 0, h))
 
     def on_core(ry, k, h):
         for rx in range(2):
@@ -204,9 +204,18 @@
 
     group_lane = lax.broadcasted_iota(jnp.int32, (group, LANES), 1)
 
+    diagonal = group_lane == lax.broadcasted_iota(jnp.int32, (group, LANES), 0)
+    comb_row = lax.broadcasted_iota(jnp.int32, (8, LANES), 0)
+
+    def swap_lanes(value):
+        even = (lax.broadcasted_iota(jnp.int32, value.shape, 1) // rows) % 2 == 0
+        swapped = jnp.where(even, pltpu.roll(value, LANES - rows, 1), pltpu.roll(value, rows, 1))
+        value = jnp.where(x == 1, swapped, value)
+        return jnp.where(core == 1, pltpu.roll(value, 2 * rows, 1), value)
+
     def scale_of(ry, k):
         aux_rows = tok_all[ry, k, :, :, :, width:].reshape(group, LANES).astype(F32)
-        return jnp.sum(jnp.where(group_lane % experts == me, aux_rows, 0.0), axis=1, keepdims=True)
+        return jnp.sum(jnp.where((group_lane % experts == me) & (group_lane < 3 * experts), aux_rows, 0.0), axis=1, keepdims=True)
 
     def forward(ry, k):
         scale = scale_of(ry, k)
@@ -240,13 +249,9 @@
 
         comb = lax.fori_loop(0, inner // TILE, step, jnp.zeros((group, 1), F32), unroll=True)
         if ry == 0:
-            high, mid, low = split3(comb)
-            columns = jnp.where(
-                group_lane == me, high,
-                jnp.where(group_lane == me + experts, mid,
-                          jnp.where(group_lane == me + 2 * experts, low, 0.0)),
-            )
-            comb_p[k] = columns.astype(BF16).reshape(2, 2, rows, LANES)
+            row = jnp.sum(jnp.where(diagonal, comb, 0.0), axis=0, keepdims=True)
+            here = jnp.where(comb_row == z_of[k], swap_lanes(row), 0.0)
+            comb_s[...] = here if k == 0 else comb_s[...] + here
 
     def out_terms(k):
         def step(j, carry):
@@ -283,38 +288,58 @@
     def x_sum(k, h):
         p, _, r, q = partial[h]
         arrived(r.at[k], "rx", k, h)
-        p[k, 0, 0] = (p[k, 0, 0].astype(F32) + r[k].astype(F32)).astype(BF16)
-        copy(p.at[k, 0, 0], q.at[k - 1], device(rz=k), ("rz", k, h), ("rz", k, h))
+        total = p[k, 0, 0].astype(F32) + r[k].astype(F32)
+        if h == 1 and k == 2:
+            arrived(q.at[2], "rz", 3, h)
+            total = total + q[2].astype(F32)
+        p[k, 0, 0] = total.astype(BF16)
+        to = 1 if h == 1 and k == 3 else k
+        copy(p.at[k, 0, 0], q.at[k - 1], device(rz=to), ("rz", k, h), ("rz", k, h))
 
     def last_sum(h):
         p, _, r, q = partial[h]
         arrived(r.at[0], "rx", 0, h)
         total = p[0, 0, 0].astype(F32) + r[0].astype(F32)
-        for k in range(1, 4):
+        for k in range(1, 3 if h == 1 else 4):
             arrived(q.at[k - 1], "rz", k, h)
             total = total + q[k - 1].astype(F32)
         return total
 
-    def comb_send():
-        copy(comb_p.at[:, 1], core_c, device(rc=1), ("cc",), ("cc",))
-
-    def comb_core():
-        arrived(core_c, "cc")
-        comb_p[:, 0] = (comb_p[:, 0].astype(F32) + core_c[...].astype(F32)).astype(BF16)
-        copy(comb_p.at[:, 0, 1], x_c, device(rx=1), ("cx",), ("cx",))
-
-    def comb_x():
-        arrived(x_c, "cx")
-        comb_p[:, 0, 0] = (comb_p[:, 0, 0].astype(F32) + x_c[...].astype(F32)).astype(BF16)
-        for k in range(1, 4):
-            copy(comb_p.at[k, 0, 0], z_c.at[k - 1], device(rz=k), ("cz", k), ("cz", k))
-
-    def comb_last():
-        total = comb_p[0, 0, 0].astype(F32)
-        for k in range(1, 4):
-            arrived(z_c.at[k - 1], "cz", k)
-            total = total + z_c[k - 1].astype(F32)
-        return total
+    hops = (
+        (combs.at[0, me], combs.at[0, me], device(rc=1)),
+        (combs.at[0, pl.ds(me - core, 2)], combs.at[0, pl.ds(me - core, 2)], device(rx=1)),
+        (combs.at[0, pl.ds(z * 4, 4)], combs.at[0, pl.ds(z * 4, 4)], device(rz=1)),
+        (combs.at[0, pl.ds(z * 4, 4)], combs.at[0, pl.ds(z * 4, 4)], device(rz=2)),
+        (combs.at[0, pl.ds(z * 4, 4)], combs.at[0, pl.ds(z * 4, 4)], device(rz=3)),
+        (combs.at[0], combs.at[1], device(ry=1)),
+    )
+
+    def hop(*steps):
+        for i in steps:
+            src, dst, to = hops[i]
+            copy(src, dst, to, ("l", i), ("l", i))
+
+    def hopped(*steps):
+        for i in steps:
+            arrived(hops[i][1], "l", i)
+
+    def logit_grads(ry, k):
+        comb = jnp.zeros((experts, LANES), F32)
+        for i in range(4):
+            comb = comb + jnp.where(z_of[k] == i, combs[ry, :, i, :], 0.0)
+        comb = swap_lanes(comb)
+        aux_t = tok_all[ry, k, :, :, :, width:].reshape(group, LANES).astype(F32).T
+        terms = [aux_t[i * experts : (i + 1) * experts, :] for i in range(6)]
+        combine = terms[0] + terms[1] + terms[2]
+        probability = terms[3] + terms[4] + terms[5]
+        selected = jnp.where(combine > 0.0, probability, 0.0)
+        sel_total = jnp.sum(selected, axis=0, keepdims=True)
+        mean = jnp.sum(combine * comb, axis=0, keepdims=True)
+        sel_grad = jnp.where(combine > 0.0, (comb - mean) / sel_total, 0.0)
+        grad = probability * (sel_grad - jnp.sum(probability * sel_grad, axis=0, keepdims=True))
+        at = (ry * 4 + k) * group
+        for i, term in enumerate(split3(grad)):
+            lgs_t[i * experts : (i + 1) * experts, at : at + group] = term.astype(BF16)
 
     def width_grads(spans, begin, end):
         def d_step(j, carry):
@@ -396,105 +421,73 @@
                 out_terms(k)
             else:
                 backward(0, k)
+                if k == 1:
+                    on_y(0, 0, TOK)
+                    on_y(0, 0, COT)
                 if k == 2:
                     core_sum(2, OUT)
                 if k == 3:
+                    combs[0, me] = comb_s[...]
+                    hop(0)
                     core_sum(3, OUT)
                     x_sum(2, OUT)
+                    hopped(0)
+                    hop(1)
                 in_terms(k)
-    comb_send()
-    for h in (TOK, COT):
-        on_y(0, h)
+    on_y(0, 1, TOK)
+    on_y(0, 1, COT)
     core_sum(3, IN)
+    for k in (1, 0):
+        core_sum(k, OUT)
+        core_sum(k, IN)
+
+    def other_plane(k):
+        for h in (TOK, COT):
+            for rx in range(2):
+                if k > 0:
+                    on_y(k, rx, h)
+        on_core(1, k, TOK)
+        forward(1, k)
+        on_core(1, k, COT)
+        backward(1, k)
+
+    other_plane(0)
     x_sum(3, OUT)
-    x_sum(2, IN)
-    comb_core()
-    core_sum(1, OUT)
-    core_sum(1, IN)
-    core_sum(0, OUT)
-    core_sum(0, IN)
-    on_core(1, 0, TOK)
-    forward(1, 0)
-    on_core(1, 0, COT)
-    backward(1, 0)
-    comb_x()
-    x_sum(3, IN)
-    for h in (TOK, COT):
-        on_y(1, h)
-    on_core(1, 1, TOK)
-    forward(1, 1)
-    on_core(1, 1, COT)
-    backward(1, 1)
-    width_grads(((0, 0, 4), (1, 0, 2)), True, False)
-    x_sum(1, OUT)
-    x_sum(1, IN)
-    inner_grads(((0, 0, 4), (1, 0, 2)), True, False)
-    for h in (TOK, COT):
-        on_y(2, h)
-    on_core(1, 2, TOK)
-    forward(1, 2)
-    on_core(1, 2, COT)
-    backward(1, 2)
-
-    comb = comb_last()
-    comb = comb + pltpu.roll(comb, LANES - experts, 1) + pltpu.roll(comb, LANES - 2 * experts, 1)
-    comb = jnp.where(first, comb, 0.0)
-    probability, chosen, combine, sel_total = small[0], small[1], small[2], small[3]
-    mean = jnp.sum(combine * comb, axis=1, keepdims=True)
-    sel_grad = jnp.where(first, chosen * (comb - mean) / sel_total, 0.0)
-    logit_grad = probability * (sel_grad - jnp.sum(probability * sel_grad, axis=1, keepdims=True))
-    high, mid, low = split3(jnp.where(first, logit_grad, 0.0))
-    mine = (high + pltpu.roll(mid, experts, 1) + pltpu.roll(low, 2 * experts, 1)).astype(BF16)
-    lgs[0, 0, 0, 0] = mine
-    hops = (
-        (lgs.at[0, 0, 0, 0], lgs.at[0, 0, 1, 0], device(rc=1)),
-        (lgs.at[0, 0, :, 0], lgs.at[0, 0, :, 1], device(rx=1)),
-        (lgs.at[0, 0], lgs.at[0, 1], device(rz=1)),
-        (lgs.at[0, 0], lgs.at[0, 2], device(rz=2)),
-        (lgs.at[0, 0], lgs.at[0, 3], device(rz=3)),
-        (lgs.at[0], lgs.at[1], device(ry=1)),
-    )
-
-    def hop(*steps):
-        for i in steps:
-            src, dst, to = hops[i]
-            copy(src, dst, to, ("l", i), ("l", i))
-
-    def hopped(*steps):
-        for i in steps:
-            arrived(hops[i][1], "l", i)
-
-    hop(0)
-    out_ref[...] = last_sum(OUT).astype(BF16)
-    on_y(3, TOK)
-    on_core(1, 3, TOK)
-    forward(1, 3)
-    hopped(0)
-    hop(1)
-    on_y(3, COT)
     hopped(1)
     hop(2, 3, 4)
-    on_core(1, 3, COT)
-    backward(1, 3)
+    x_sum(3, IN)
+    other_plane(1)
+    x_sum(1, OUT)
+    other_plane(2)
+    x_sum(2, IN)
+    width_grads(((0, 0, 4),), True, False)
+    x_sum(1, IN)
+    hopped(2, 3, 4)
+    hop(5)
+    inner_grads(((0, 0, 4),), True, False)
+    for k in range(4):
+        logit_grads(0, k)
+    other_plane(3)
+    out_ref[...] = last_sum(OUT).astype(BF16)
     stores = [
         pltpu.make_async_copy(src, dst, store_sem.at[i])
         for i, (src, dst) in enumerate(((gg_ref, gg_hbm), (ug_ref, ug_hbm), (dg_ref, dg_hbm)))
     ]
-    width_grads(((1, 2, 4),), False, True)
+    width_grads(((1, 0, 4),), False, True)
     stores[0].start()
     stores[1].start()
-    hopped(2, 3, 4)
-    hop(5)
-    inner_grads(((1, 2, 4),), False, True)
+    inner_grads(((1, 0, 4),), False, True)
     stores[2].start()
-    tgrad_ref[...] = (last_sum(IN) + dot(mine, router_t[...], NN)).astype(BF16)
+    back = dot(lgs_t[: 3 * experts, :group], router_t[: 3 * experts, :], TN)
+    tgrad_ref[...] = (last_sum(IN) + back[:rows]).astype(BF16)
     hopped(5)
-    lgs_t[...] = lgs[...].reshape(32 * rows, LANES).astype(F32).T.astype(BF16)
+    for k in range(4):
+        logit_grads(1, k)
 
     def r_step(j, carry):
         cols = pl.ds(pl.multiple_of(j * TILE, TILE), TILE)
         total = dot(
-            lgs_t[: 3 * experts, :], tok_all[:, :, :, :, :, cols].reshape(32 * rows, TILE), NN
+            lgs_t[...], tok_all[:, :, :, :, :, cols].reshape(32 * rows, TILE), NN
         )
         rgrad_ref[:, cols] = (
             total[:experts] + total[experts : 2 * experts] + total[2 * experts : 3 * experts]
@@ -577,14 +570,14 @@
         vmem(8, 4 * rows, inner), vmem(8, 4 * rows, inner), vmem(8, 4 * rows, inner),
         vmem(4 * rows, inner, dtype=F32), vmem(4 * rows, inner, dtype=F32),
         vmem(4 * rows, inner, dtype=F32),
-        vmem(4, 2, 2, rows, width), vmem(4, 2, 2, rows, width), vmem(4, 2, 2, rows, LANES),
-        vmem(4, 2, rows, width), vmem(4, 2, rows, width), vmem(4, 2, rows, LANES),
-        vmem(4, rows, width), vmem(4, rows, width), vmem(4, rows, LANES),
-        vmem(3, rows, width), vmem(3, rows, width), vmem(3, rows, LANES),
-        vmem(2, 4, 2, 2, rows, LANES), vmem(LANES, 32 * rows), vmem(LANES, width),
+        vmem(4, 2, 2, rows, width), vmem(4, 2, 2, rows, width),
+        vmem(4, 2, rows, width), vmem(4, 2, rows, width),
+        vmem(4, rows, width), vmem(4, rows, width),
+        vmem(3, rows, width), vmem(3, rows, width),
+        vmem(2, experts, 8, LANES, dtype=F32), vmem(8, LANES, dtype=F32),
+        vmem(3 * experts, 32 * rows), vmem(LANES, width),
         vmem(half, inner, dtype=F32), vmem(half, inner, dtype=F32), vmem(inner, half, dtype=F32),
         vmem(half, inner), vmem(half, inner), vmem(inner, half),
-        vmem(4, rows, LANES, dtype=F32),
         pltpu.SemaphoreType.DMA((3,)), pltpu.SemaphoreType.DMA((3,)),
         pltpu.SemaphoreType.DMA((2 * COPIES,)), pltpu.SemaphoreType.DMA((2 * COPIES,)),
     ]

time: 87.6 us -> 74.5 us (0.85); the launches traced: 86.6 us -> 74.4 us
  Pallas kernels: 85.8 us -> 73.6 us
    pallas_call x1, Pallas kernels: 80.9 us -> 68.7 us  [local_fused(): pl.pallas_call(functools.partial(fused, experts), out_shape=(jax.ShapeDty...]
where the time goes in v3:
time: 74.5 us; the launch traced here: 74.4 us
  Pallas kernels  73.6 us (99%)
  between operations  0.82 us (1%)
    pallas_call x1, Pallas kernels, local_fused(): pl.pallas_call(functools.partial(fused, experts), out_shape=(jax.ShapeDty...  68.7 us
    pallas_call x1, Pallas kernels, hand_over(): pl.pallas_call(kernel, out_shape=tuple((jax.ShapeDtypeStruct(a.shape, a.d...  4.91 us

profile of v3, /device:TPU:1, one launch (start us, length us, event | category | flops | bytes accessed | tf_op | source)
XLA Modules:
  0.0 74.4 jit_solution(16212566133777592049)
XLA Ops:
  0.6 68.7 %shard_map.118 = (bf16[32,2048]{1,0:T(8,128)(2,1)}, bf16[32,2048]{1,0:T(8,128)(2,1)}, bf16[1024,768]{1,0:T(8,128)(2,1)}, bf16[1024,768]{1,0:T(8,128)(2,1)}, bf16...) custom-call(bf16[32,2048]{1,0:T(8,128)(2,1)} %tok_ref.1, s32[8,32]{1,0:T(8,128)} %bitcast.13, bf16[32,2048]{1,0:T(8,128)(2,1)} %cot_ref.1, ...), custom_call_target="tpu_custom_call" | custom-call | tf_op jit(solution)/shard_map/pallas_call | solution.py:586
  69.3 4.9 %shard_map.119 = (bf16[32,2048]{1,0:T(8,128)(2,1)}, bf16[32,2048]{1,0:T(8,128)(2,1)}, bf16[1024,768]{1,0:T(8,128)(2,1)}, bf16[1024,768]{1,0:T(8,128)(2,1)}, bf16...) custom-call(bf16[32,2048]{1,0:T(8,128)(2,1)} %get-tuple-element.18.refs_0_, bf16[32,2048]{1,0:T(8,128)(2,1)} %get-tuple-element.19.refs_1_, ...), custom_call_target="tpu_custom_call" | custom-call | tf_op jit(solution)/shard_map/pallas_call | solution.py:548

commit v4 on v3

--- a/solution.py
+++ b/solution.py
@@ -478,8 +478,6 @@
     stores[1].start()
     inner_grads(((1, 0, 4),), False, True)
     stores[2].start()
-    back = dot(lgs_t[: 3 * experts, :group], router_t[: 3 * experts, :], TN)
-    tgrad_ref[...] = (last_sum(IN) + back[:rows]).astype(BF16)
     hopped(5)
     for k in range(4):
         logit_grads(1, k)
@@ -496,6 +494,8 @@
 
     lax.fori_loop(0, width // TILE, r_step, 0, unroll=True)
 
+    back = dot(lgs_t[: 3 * experts, :group], router_t[: 3 * experts, :], TN)
+    tgrad_ref[...] = (last_sum(IN) + back[:rows]).astype(BF16)
     for store in stores:
         store.wait()
     for made in sent:
@@ -525,18 +525,13 @@
 
 def hand_over(arrays):
     n = len(arrays)
-    pieces = [4 if a.shape[0] >= 128 else 2 for a in arrays]
+    order = sorted(range(n), key=lambda i: -arrays[i].size)
 
     def kernel(*refs):
         sources, targets, held = refs[:n], refs[n : 2 * n], refs[2 * n : 3 * n]
         in_sem, out_sem = refs[3 * n :]
-        ins, outs = [], []
-        for i in range(n):
-            step = arrays[i].shape[0] // pieces[i]
-            for j in range(pieces[i]):
-                at = pl.ds(j * step, step)
-                ins.append(pltpu.make_async_copy(sources[i].at[at], held[i].at[at], in_sem.at[i, j]))
-                outs.append(pltpu.make_async_copy(held[i].at[at], targets[i].at[at], out_sem.at[i, j]))
+        ins = [pltpu.make_async_copy(sources[i], held[i], in_sem.at[i]) for i in order]
+        outs = [pltpu.make_async_copy(held[i], targets[i], out_sem.at[i]) for i in order]
         for made in ins:
             made.start()
         for before, made in zip(ins, outs):
@@ -551,7 +546,7 @@
         in_specs=[pl.BlockSpec(memory_space=pl.ANY)] * n,
         out_specs=(pl.BlockSpec(memory_space=pl.ANY),) * n,
         scratch_shapes=[pltpu.VMEM(a.shape, a.dtype) for a in arrays]
-        + [pltpu.SemaphoreType.DMA((n, 4)), pltpu.SemaphoreType.DMA((n, 4))],
+        + [pltpu.SemaphoreType.DMA((n,)), pltpu.SemaphoreType.DMA((n,))],
         compiler_params=pltpu.CompilerParams(vmem_limit_bytes=60 * 2**20),
     )(*arrays)
 

time: 74.5 us -> 73.4 us (0.985)
  Pallas kernels: 73.6 us -> 72.5 us
    pallas_call x1, Pallas kernels: 4.91 us -> 3.8 us  [hand_over(): pl.pallas_call(kernel, out_shape=tuple((jax.ShapeDtypeStruct(a.shape, a.d...]
where the time goes in v4:
time: 73.4 us; the launch traced here: 73.3 us
  Pallas kernels  72.5 us (99%)
  between operations  0.82 us (1%)
    pallas_call x1, Pallas kernels, local_fused(): pl.pallas_call(functools.partial(fused, experts), out_shape=(jax.ShapeDty...  68.7 us
    pallas_call x1, Pallas kernels, hand_over(): pl.pallas_call(kernel, out_shape=tuple((jax.ShapeDtypeStruct(a.shape, a.d...  3.8 us

profile of v4, /device:TPU:1, one launch (start us, length us, event | category | flops | bytes accessed | tf_op | source)
XLA Modules:
  0.0 73.3 jit_solution(16537853509061421216)
XLA Ops:
  0.6 68.7 %shard_map.118 = (bf16[32,2048]{1,0:T(8,128)(2,1)}, bf16[32,2048]{1,0:T(8,128)(2,1)}, bf16[1024,768]{1,0:T(8,128)(2,1)}, bf16[1024,768]{1,0:T(8,128)(2,1)}, bf16...) custom-call(bf16[32,2048]{1,0:T(8,128)(2,1)} %tok_ref.1, s32[8,32]{1,0:T(8,128)} %bitcast.13, bf16[32,2048]{1,0:T(8,128)(2,1)} %cot_ref.1, ...), custom_call_target="tpu_custom_call" | custom-call | tf_op jit(solution)/shard_map/pallas_call | solution.py:581
  69.3 3.8 %shard_map.119 = (bf16[32,2048]{1,0:T(8,128)(2,1)}, bf16[32,2048]{1,0:T(8,128)(2,1)}, bf16[1024,768]{1,0:T(8,128)(2,1)}, bf16[1024,768]{1,0:T(8,128)(2,1)}, bf16...) custom-call(bf16[32,2048]{1,0:T(8,128)(2,1)} %get-tuple-element.18.refs_0_, bf16[32,2048]{1,0:T(8,128)(2,1)} %get-tuple-element.19.refs_1_, ...), custom_call_target="tpu_custom_call" | custom-call | tf_op jit(solution)/shard_map/pallas_call | solution.py:543
